TPU v7x, 512 devices: a whole 4x8x8 slice. The times are simulated.
512 devices in a mesh: seq: 64 (over z, x, y_lo), tensor: 8 (over y_hi, core).
Axes of the slice: x: 4, y: 8 (y_hi: 4, y_lo: 2; y = y_hi * 2 + y_lo), z: 8, core: 2. Of those that a mesh axis runs over, the one named last changes fastest.
Arguments:
- hidden_in: bfloat16 [8192, 8192], P('seq', 'tensor'), may hold values from -6 to 6
- query_base: bfloat16 [8192, 8192], P('seq', 'tensor'), may hold values from -6 to 6
- key_proj: bfloat16 [8192, 1024], P('seq', 'tensor'), may hold values from -6 to 6
- frozen_value_output: bfloat16 [8192, 1024], P('seq', 'tensor'), may hold values from -24 to 24
- down_query: bfloat16 [8, 8192], P(None, 'tensor'), may hold values from -0.0625 to 0.0625
- up_query: bfloat16 [8, 8192], P(None, 'tensor'), may hold values from -0.625 to 0.625
- down_value: bfloat16 [8, 8192], P(None, 'tensor'), may hold values from -0.0625 to 0.0625
- value_up_weight: bfloat16 [8, 1024], P(None, 'tensor'), may hold values from -0.625 to 0.625
- grad_out: bfloat16 [8192, 8192], P('seq', 'tensor'), may hold values from -0.0625 to 0.0625
Outputs:
- attended: bfloat16 [8192, 8192], P('seq', 'tensor')
- grad_down_query: float32 [8, 8192], P(None, 'tensor')
- grad_up_query: float32 [8, 8192], P(None, 'tensor')
- grad_down_value: float32 [8, 8192], P(None, 'tensor')
- grad_up_value: float32 [8, 1024], P(None, 'tensor')
All inputs are finite; a program needn't handle non-finite values.
Results may differ from a plain program's by a relative error of at most 0.017.
Values may be sent and summed in bfloat16 or wider, within the bound.
A program may use at most 64 MiB of HBM per device.

v0:
```python
import jax
import jax.numpy as jnp
from jax import lax
from jax.sharding import PartitionSpec as P

QUERY_HEADS = 64
KEY_VALUE_HEADS = 8
HEAD_SIZE = 128
GROUP_TOKENS = 2048


adapter_gain = 2.0


def shifted_2(value, axis, steps):
    count = lax.axis_size(axis)
    pairs = [(source, (source + steps) % count) for source in range(count)]
    return lax.ppermute(value, axis, pairs)


def per_device(
    hidden_in,
    query_base,
    key_proj,
    frozen_value_output,
    down_query,
    up_query,
    down_value,
    value_up_weight,
    grad_out,
):
    tok_rows = hidden_in.shape[0]
    group_devs = GROUP_TOKENS // tok_rows
    local_kv = key_proj.shape[1] // HEAD_SIZE
    repeat_count = QUERY_HEADS // KEY_VALUE_HEADS
    head_block = min(repeat_count, max(1, 512 // tok_rows))
    inv_root = HEAD_SIZE ** (-0.5)
    highest = lax.Precision.HIGHEST
    contract_last = (((1,), (1,)), ((), ()))
    first_dims = (((0,), (0,)), ((), ()))
    part_query = lax.dot_general(
        hidden_in, down_query, contract_last, preferred_element_type=jnp.float32
    )
    part_value = lax.dot_general(
        hidden_in, down_value, contract_last, preferred_element_type=jnp.float32
    )
    low_query, low_value = lax.psum((part_query, part_value), "tensor")
    query = (
        query_base.astype(jnp.float32)
        + adapter_gain * jnp.dot(low_query, up_query.astype(jnp.float32), precision=highest)
    ).astype(jnp.bfloat16)
    value = (
        frozen_value_output.astype(jnp.float32)
        + adapter_gain * jnp.dot(low_value, value_up_weight.astype(jnp.float32), precision=highest)
    ).astype(jnp.bfloat16)
    stacked = jnp.stack([key_proj, value], axis=0)
    received = [stacked]
    for shift_offset in range(1, group_devs):
        received.append(shifted_2(stacked, "seq", shift_offset))
    ordered = jnp.concatenate(received[::-1], axis=1)
    seq_index = lax.axis_index("seq")
    seq_count = lax.axis_size("seq")
    shifted = lax.axis_index("tensor") >= lax.axis_size("tensor") // 2
    lag_devs = jnp.where(shifted, group_devs // 2, 0)
    group_place = (seq_index - lag_devs) % seq_count % group_devs
    column = lax.broadcasted_iota(jnp.int32, (tok_rows, group_devs * tok_rows), 1)
    row_pos = lax.broadcasted_iota(jnp.int32, (tok_rows, group_devs * tok_rows), 0)
    block_of = column // tok_rows
    allowed = (block_of >= group_devs - 1 - group_place) & (
        (block_of < group_devs - 1) | (column % tok_rows <= row_pos)
    )
    query_heads = query.reshape(tok_rows, local_kv, repeat_count, HEAD_SIZE)
    cot_heads = grad_out.reshape(tok_rows, local_kv, repeat_count, HEAD_SIZE)
    key_head = ordered[0, :, 0:HEAD_SIZE]
    value_head = ordered[1, :, 0:HEAD_SIZE]
    value_grad = jnp.zeros((group_devs * tok_rows, HEAD_SIZE), jnp.float32)
    out_parts = []
    grad_parts = []
    for head_start in range(0, repeat_count, head_block):
        query_part = query_heads[:, 0, head_start : head_start + head_block, :]
        cot_part = cot_heads[:, 0, head_start : head_start + head_block, :]
        scores = (
            jnp.einsum("thd,cd->htc", query_part, key_head, preferred_element_type=jnp.float32)
            * inv_root
        )
        masked = jnp.where(allowed, scores, -jnp.inf)
        row_max = jnp.max(masked, axis=-1, keepdims=True)
        exp_terms = jnp.exp(masked - row_max)
        soft_weights = exp_terms / jnp.sum(exp_terms, axis=-1, keepdims=True)
        rounded = soft_weights.astype(jnp.bfloat16)
        output = jnp.einsum("htc,cd->thd", rounded, value_head, preferred_element_type=jnp.float32)
        value_grad = value_grad + jnp.einsum(
            "htc,thd->cd", rounded, cot_part, preferred_element_type=jnp.float32
        )
        grad_probs = jnp.einsum(
            "thd,cd->htc", cot_part, value_head, preferred_element_type=jnp.float32
        )
        center = jnp.sum(soft_weights * grad_probs, axis=-1, keepdims=True)
        grad_scores = (soft_weights * (grad_probs - center)).astype(jnp.bfloat16)
        grad_query = (
            jnp.einsum("htc,cd->thd", grad_scores, key_head, preferred_element_type=jnp.float32)
            * inv_root
        )
        out_parts.append(output.astype(jnp.bfloat16))
        grad_parts.append(grad_query)
    out_heads = [jnp.concatenate(out_parts, axis=1)]
    grad_heads = [jnp.concatenate(grad_parts, axis=1)]
    value_heads = [value_grad]
    attended = jnp.stack(out_heads, axis=1).reshape(tok_rows, local_kv * repeat_count * HEAD_SIZE)
    d_query = jnp.stack(grad_heads, axis=1).reshape(tok_rows, local_kv * repeat_count * HEAD_SIZE)
    value_blocks = jnp.stack(value_heads, axis=1).reshape(
        group_devs, tok_rows, local_kv * HEAD_SIZE
    )
    d_value = value_blocks[group_devs - 1]
    for shift_offset in range(1, group_devs):
        d_value = d_value + shifted_2(
            value_blocks[group_devs - 1 - shift_offset].astype(jnp.bfloat16), "seq", -shift_offset
        ).astype(jnp.float32)
    grad_up_query = adapter_gain * jnp.dot(low_query.T, d_query, precision=highest)
    grad_up_value = adapter_gain * jnp.dot(low_value.T, d_value, precision=highest)
    part_grad_query = adapter_gain * jnp.dot(
        d_query, up_query.astype(jnp.float32).T, precision=highest
    )
    part_grad_value = adapter_gain * jnp.dot(
        d_value, value_up_weight.astype(jnp.float32).T, precision=highest
    )
    low_grad_query, low_grad_value = lax.psum((part_grad_query, part_grad_value), "tensor")
    down_grad_query = lax.dot_general(
        low_grad_query.astype(jnp.bfloat16),
        hidden_in,
        first_dims,
        preferred_element_type=jnp.float32,
    )
    down_grad_value = lax.dot_general(
        low_grad_value.astype(jnp.bfloat16),
        hidden_in,
        first_dims,
        preferred_element_type=jnp.float32,
    )
    totals = lax.psum((down_grad_query, grad_up_query, down_grad_value, grad_up_value), "seq")
    return (attended, totals[0], totals[1], totals[2], totals[3])


def solution(mesh):
    return jax.shard_map(
        per_device,
        mesh=mesh,
        in_specs=(
            P("seq", "tensor"),
            P("seq", "tensor"),
            P("seq", "tensor"),
            P("seq", "tensor"),
            P(None, "tensor"),
            P(None, "tensor"),
            P(None, "tensor"),
            P(None, "tensor"),
            P("seq", "tensor"),
        ),
        out_specs=(
            P("seq", "tensor"),
            P(None, "tensor"),
            P(None, "tensor"),
            P(None, "tensor"),
            P(None, "tensor"),
        ),
        check_vma=False,
    )
```

profile of v0, /device:TPU:6, one launch (start us, length us, event | category | flops | bytes accessed | tf_op | source)
XLA Modules:
  0.0 833.8 jit_solution(1315904959098317824)
XLA Ops:
  9.9 18.2 %all-reduce.2 = (f32[128,8]{0,1:T(8,128)S(1)}, f32[128,8]{0,1:T(8,128)S(1)}) all-reduce(f32[128,8]{0,1:T(8,128)S(1)} %fusion.90, f32[128,8]{0,1:T(8,128)S(1)} %fusion.91), channel_id=1, replica_groups=mesh['seq'=64,'tensor'=8] {'tensor'}, use_global_device_ids=true, to_apply=%region_0.0 | all-reduce | flops 2048 | bytes 16384 | tf_op jit(solution)/shard_map/psum | solution.py:47
  29.9 2.6 collective-permute-start.14
  32.5 4.2 collective-permute-start.13
  36.7 5.1 collective-permute-start.12
  41.8 4.8 collective-permute-start.11
  46.6 5.4 collective-permute-start
  53.5 2.5 fusion.48
  57.4 6.6 collective-permute-start.1
  64.0 2.9 collective-permute-done.1
  66.9 6.5 collective-permute-start.2
  73.4 3.8 collective-permute-done.2
  77.2 4.2 collective-permute-start.3
  81.4 5.5 collective-permute-done.3
  87.0 5.9 collective-permute-start.4
  92.9 4.8 collective-permute-done.4
  97.8 4.0 collective-permute-start.5
  101.8 4.2 collective-permute-done.5
  106.0 3.9 collective-permute-start.6
  110.0 5.2 collective-permute-done.6
  115.2 4.0 collective-permute-start.7
  119.2 3.3 collective-permute-done.7
  122.6 4.8 collective-permute-start.8
  127.3 4.4 collective-permute-done.8
  133.7 9.6 %collective-permute-done.9 = bf16[2,128,128]{2,1,0:T(8,128)(2,1)S(1)} collective-permute-done((bf16[2,128,128]{2,1,0:T(8,128)(2,1)S(1)}, bf16[2,128,128]{2,1,0:T(8,128)(2,1)S(1)}, u32[]{:S(2)}, u32[]{:S(2)}) %collective-permute-start.9) | collective-permute-done | bytes 65568 | tf_op jit(solution)/shard_map/ppermute | solution.py:18
  143.3 4.3 collective-permute-start.10
  147.5 5.7 collective-permute-done.10
  153.4 3.3 fusion.87
  158.8 3.4 convolution_bitcast_fusion
  162.2 4.8 fusion.2
  167.0 3.3 fusion.88
  172.4 4.9 fusion.5
  177.3 3.5 fusion.89
  182.8 5.4 collective-permute-start.29
  188.2 5.9 collective-permute-start.28
  194.1 7.3 collective-permute-start.27
  203.4 4.8 fusion.29
  208.2 4.8 fusion.35
  213.1 4.5 collective-permute-start.25
  219.6 5.0 collective-permute-start.23
  224.6 4.2 collective-permute-start.22
  231.9 5.3 collective-permute-start.20
  237.2 6.3 collective-permute-start.19
  243.5 3.2 collective-permute-start.18
  246.7 3.6 collective-permute-start.17
  250.3 2.7 collective-permute-start.16
  255.5 2.7 collective-permute-done.16
  259.2 28.3 %all-reduce.1 = (bf16[128,8]{1,0:T(8,128)(2,1)S(1)}, bf16[128,8]{1,0:T(8,128)(2,1)S(1)}) all-reduce(f32[128,8]{1,0:T(8,128)S(1)} %convolution_multiply_fusion.3, f32[128,8]{1,0:T(8,128)S(1)} %convolution_multiply_fusion.1), channel_id=1, replica_groups=mesh['seq'=64,'tensor'=8] {'tensor'}, use_global_device_ids=true, to_apply=%region_8.9 | all-reduce | flops 2048 | bytes 12288 | tf_op jit(solution)/shard_map/psum | solution.py:127
  290.1 531.4 %all-reduce.5.cloned.1.call-done = (f32[8,1024]{1,0:T(8,128)}, f32[8,1024]{1,0:T(8,128)}, f32[8,1024]{1,0:T(8,128)}, f32[8,128]{1,0:T(8,128)}) async-done(((f32[8,1024]{1,0:T(8,128)}, f32[8,1024]{1,0:T(8,128)}, f32[8,1024]{1,0:T(8,128)}, f32[8,128]{1,0:T(8,128)}), (f32[8,1024]{1,0:T(8,128)}, f32[8,1024]{1,0:T(8,128)}, f32[8,1024]{1,0:T(8,128)}, f32[8,128]{1,0:T(8,128)})) %all-reduce.5.cloned.1.call-update) | async-done | bytes 102416 | tf_op jit(solution)/shard_map/psum | solution.py:140
  (80 shorter events, 34.0 us)
Async XLA Ops:
  7.2 1.0 copy-start
  7.2 146.2 %copy-start.1 = (bf16[128,128]{1,0:T(8,128)(2,1)S(1)}, bf16[128,128]{1,0:T(8,128)(2,1)}, u32[]{:S(2)}) copy-start(bf16[128,128]{1,0:T(8,128)(2,1)} %param.11) | copy-start | bytes 98308
  7.2 814.4 %all-reduce.5.cloned.1.call-start = ((), (), s32[]{:S(2)}) async-start(), calls=%async_computation | async-start | bytes 204800 | tf_op jit(solution)/shard_map/psum | solution.py:140
  29.9 123.5 %collective-permute-start.14 = (bf16[2,128,128]{2,1,0:T(8,128)(2,1)S(1)}, bf16[2,128,128]{2,1,0:T(8,128)(2,1)S(1)}, u32[]{:S(2)}, u32[]{:S(2)}) collective-permute-start(bf16[2,128,128]{2,1,0:T(8,128)(2,1)S(1)} %pad_maximum_fusion.2), channel_id=1, source_target_pairs={{0,8},{8,16},{16,24},{24,32},{32,40},{40,48},{48,56},{56,64},{64,7... | collective-permute-start | bytes 196616 | tf_op jit(solution)/shard_map/ppermute | solution.py:18
  32.5 120.8 %collective-permute-start.13 = (bf16[2,128,128]{2,1,0:T(8,128)(2,1)S(1)}, bf16[2,128,128]{2,1,0:T(8,128)(2,1)S(1)}, u32[]{:S(2)}, u32[]{:S(2)}) collective-permute-start(bf16[2,128,128]{2,1,0:T(8,128)(2,1)S(1)} %pad_maximum_fusion.2), channel_id=1, source_target_pairs={{0,16},{8,24},{16,32},{24,40},{32,48},{40,56},{48,64},{56,72},{64,... | collective-permute-start | bytes 196616 | tf_op jit(solution)/shard_map/ppermute | solution.py:18
  36.7 116.6 %collective-permute-start.12 = (bf16[2,128,128]{2,1,0:T(8,128)(2,1)S(1)}, bf16[2,128,128]{2,1,0:T(8,128)(2,1)S(1)}, u32[]{:S(2)}, u32[]{:S(2)}) collective-permute-start(bf16[2,128,128]{2,1,0:T(8,128)(2,1)S(1)} %pad_maximum_fusion.2), channel_id=1, source_target_pairs={{0,24},{8,32},{16,40},{24,48},{32,56},{40,64},{48,72},{56,80},{64,... | collective-permute-start | bytes 196616 | tf_op jit(solution)/shard_map/ppermute | solution.py:18
  41.8 111.5 %collective-permute-start.11 = (bf16[2,128,128]{2,1,0:T(8,128)(2,1)S(1)}, bf16[2,128,128]{2,1,0:T(8,128)(2,1)S(1)}, u32[]{:S(2)}, u32[]{:S(2)}) collective-permute-start(bf16[2,128,128]{2,1,0:T(8,128)(2,1)S(1)} %pad_maximum_fusion.2), channel_id=1, source_target_pairs={{0,32},{8,40},{16,48},{24,56},{32,64},{40,72},{48,80},{56,88},{64,... | collective-permute-start | bytes 196616 | tf_op jit(solution)/shard_map/ppermute | solution.py:18
  46.6 10.8 %collective-permute-start = (bf16[2,128,128]{2,1,0:T(8,128)(2,1)S(1)}, bf16[2,128,128]{2,1,0:T(8,128)(2,1)S(1)}, u32[]{:S(2)}, u32[]{:S(2)}) collective-permute-start(bf16[2,128,128]{2,1,0:T(8,128)(2,1)S(1)} %pad_maximum_fusion.2), channel_id=1, source_target_pairs={{0,120},{8,128},{16,136},{24,144},{32,152},{40,160},{48,168},{56,1... | collective-permute-start | bytes 196616 | tf_op jit(solution)/shard_map/ppermute | solution.py:18
  57.4 9.5 %collective-permute-start.1 = (bf16[2,128,128]{2,1,0:T(8,128)(2,1)S(1)}, bf16[2,128,128]{2,1,0:T(8,128)(2,1)S(1)}, u32[]{:S(2)}, u32[]{:S(2)}) collective-permute-start(bf16[2,128,128]{2,1,0:T(8,128)(2,1)S(1)} %pad_maximum_fusion.2), channel_id=1, source_target_pairs={{0,112},{8,120},{16,128},{24,136},{32,144},{40,152},{48,160},{56,1... | collective-permute-start | bytes 196616 | tf_op jit(solution)/shard_map/ppermute | solution.py:18
  66.9 10.4 %collective-permute-start.2 = (bf16[2,128,128]{2,1,0:T(8,128)(2,1)S(1)}, bf16[2,128,128]{2,1,0:T(8,128)(2,1)S(1)}, u32[]{:S(2)}, u32[]{:S(2)}) collective-permute-start(bf16[2,128,128]{2,1,0:T(8,128)(2,1)S(1)} %pad_maximum_fusion.2), channel_id=1, source_target_pairs={{0,104},{8,112},{16,120},{24,128},{32,136},{40,144},{48,152},{56,1... | collective-permute-start | bytes 196616 | tf_op jit(solution)/shard_map/ppermute | solution.py:18
  77.2 9.8 %collective-permute-start.3 = (bf16[2,128,128]{2,1,0:T(8,128)(2,1)S(1)}, bf16[2,128,128]{2,1,0:T(8,128)(2,1)S(1)}, u32[]{:S(2)}, u32[]{:S(2)}) collective-permute-start(bf16[2,128,128]{2,1,0:T(8,128)(2,1)S(1)} %pad_maximum_fusion.2), channel_id=1, source_target_pairs={{0,96},{8,104},{16,112},{24,120},{32,128},{40,136},{48,144},{56,15... | collective-permute-start | bytes 196616 | tf_op jit(solution)/shard_map/ppermute | solution.py:18
  87.0 10.8 %collective-permute-start.4 = (bf16[2,128,128]{2,1,0:T(8,128)(2,1)S(1)}, bf16[2,128,128]{2,1,0:T(8,128)(2,1)S(1)}, u32[]{:S(2)}, u32[]{:S(2)}) collective-permute-start(bf16[2,128,128]{2,1,0:T(8,128)(2,1)S(1)} %pad_maximum_fusion.2), channel_id=1, source_target_pairs={{0,88},{8,96},{16,104},{24,112},{32,120},{40,128},{48,136},{56,144... | collective-permute-start | bytes 196616 | tf_op jit(solution)/shard_map/ppermute | solution.py:18
  97.8 8.3 collective-permute-start.5
  106.0 9.2 %collective-permute-start.6 = (bf16[2,128,128]{2,1,0:T(8,128)(2,1)S(1)}, bf16[2,128,128]{2,1,0:T(8,128)(2,1)S(1)}, u32[]{:S(2)}, u32[]{:S(2)}) collective-permute-start(bf16[2,128,128]{2,1,0:T(8,128)(2,1)S(1)} %pad_maximum_fusion.2), channel_id=1, source_target_pairs={{0,72},{8,80},{16,88},{24,96},{32,104},{40,112},{48,120},{56,128},... | collective-permute-start | bytes 196616 | tf_op jit(solution)/shard_map/ppermute | solution.py:18
  115.2 7.4 collective-permute-start.7
  122.6 9.2 %collective-permute-start.8 = (bf16[2,128,128]{2,1,0:T(8,128)(2,1)S(1)}, bf16[2,128,128]{2,1,0:T(8,128)(2,1)S(1)}, u32[]{:S(2)}, u32[]{:S(2)}) collective-permute-start(bf16[2,128,128]{2,1,0:T(8,128)(2,1)S(1)} %pad_maximum_fusion.2), channel_id=1, source_target_pairs={{0,56},{8,64},{16,72},{24,80},{32,88},{40,96},{48,104},{56,112},{6... | collective-permute-start | bytes 196616 | tf_op jit(solution)/shard_map/ppermute | solution.py:18
  131.7 11.6 %collective-permute-start.9 = (bf16[2,128,128]{2,1,0:T(8,128)(2,1)S(1)}, bf16[2,128,128]{2,1,0:T(8,128)(2,1)S(1)}, u32[]{:S(2)}, u32[]{:S(2)}) collective-permute-start(bf16[2,128,128]{2,1,0:T(8,128)(2,1)S(1)} %pad_maximum_fusion.2), channel_id=1, source_target_pairs={{0,48},{8,56},{16,64},{24,72},{32,80},{40,88},{48,96},{56,104},{64... | collective-permute-start | bytes 196616 | tf_op jit(solution)/shard_map/ppermute | solution.py:18
  143.3 10.0 %collective-permute-start.10 = (bf16[2,128,128]{2,1,0:T(8,128)(2,1)S(1)}, bf16[2,128,128]{2,1,0:T(8,128)(2,1)S(1)}, u32[]{:S(2)}, u32[]{:S(2)}) collective-permute-start(bf16[2,128,128]{2,1,0:T(8,128)(2,1)S(1)} %pad_maximum_fusion.2), channel_id=1, source_target_pairs={{0,40},{8,48},{16,56},{24,64},{32,72},{40,80},{48,88},{56,96},{64,... | collective-permute-start | bytes 196616 | tf_op jit(solution)/shard_map/ppermute | solution.py:18
  153.4 19.0 %copy-start.4 = (bf16[2,2048,128]{2,1,0:T(8,128)(2,1)}, bf16[2,2048,128]{2,1,0:T(8,128)(2,1)S(1)}, u32[]{:S(2)}) copy-start(bf16[2,2048,128]{2,1,0:T(8,128)(2,1)S(1)} %constant_dynamic-update-slice_fusion) | copy-start | bytes 3145732
  180.8 32.3 %collective-permute-start.15 = (bf16[128,128]{1,0:T(8,128)(2,1)S(1)}, bf16[128,128]{1,0:T(8,128)(2,1)S(1)}, u32[]{:S(2)}, u32[]{:S(2)}) collective-permute-start(bf16[128,128]{1,0:T(8,128)(2,1)S(1)} %get-tuple-element.23), channel_id=1, source_target_pairs={{0,504},{8,0},{16,8},{24,16},{32,24},{40,32},{48,40},{56,48},{64,5... | collective-permute-start | bytes 98312 | tf_op jit(solution)/shard_map/ppermute | solution.py:18
  182.8 34.8 %collective-permute-start.29 = (bf16[128,128]{1,0:T(8,128)(2,1)S(1)}, bf16[128,128]{1,0:T(8,128)(2,1)S(1)}, u32[]{:S(2)}, u32[]{:S(2)}) collective-permute-start(bf16[128,128]{1,0:T(8,128)(2,1)S(1)} %get-tuple-element.24), channel_id=1, source_target_pairs={{0,392},{8,400},{16,408},{24,416},{32,424},{40,432},{48,440},{56,4... | collective-permute-start | bytes 98312 | tf_op jit(solution)/shard_map/ppermute | solution.py:18
  188.2 31.4 %collective-permute-start.28 = (bf16[128,128]{1,0:T(8,128)(2,1)S(1)}, bf16[128,128]{1,0:T(8,128)(2,1)S(1)}, u32[]{:S(2)}, u32[]{:S(2)}) collective-permute-start(bf16[128,128]{1,0:T(8,128)(2,1)S(1)} %get-tuple-element.25), channel_id=1, source_target_pairs={{0,400},{8,408},{16,416},{24,424},{32,432},{40,440},{48,448},{56,4... | collective-permute-start | bytes 98312 | tf_op jit(solution)/shard_map/ppermute | solution.py:18
  194.1 30.5 %collective-permute-start.27 = (bf16[128,128]{1,0:T(8,128)(2,1)S(1)}, bf16[128,128]{1,0:T(8,128)(2,1)S(1)}, u32[]{:S(2)}, u32[]{:S(2)}) collective-permute-start(bf16[128,128]{1,0:T(8,128)(2,1)S(1)} %get-tuple-element.26), channel_id=1, source_target_pairs={{0,408},{8,416},{16,424},{24,432},{32,440},{40,448},{48,456},{56,4... | collective-permute-start | bytes 98312 | tf_op jit(solution)/shard_map/ppermute | solution.py:18
  201.5 27.3 %collective-permute-start.26 = (bf16[128,128]{1,0:T(8,128)(2,1)S(1)}, bf16[128,128]{1,0:T(8,128)(2,1)S(1)}, u32[]{:S(2)}, u32[]{:S(2)}) collective-permute-start(bf16[128,128]{1,0:T(8,128)(2,1)S(1)} %get-tuple-element.27), channel_id=1, source_target_pairs={{0,416},{8,424},{16,432},{24,440},{32,448},{40,456},{48,464},{56,4... | collective-permute-start | bytes 98312 | tf_op jit(solution)/shard_map/ppermute | solution.py:18
  208.2 23.0 %copy-start.2 = (bf16[8,1024]{1,0:T(8,128)(2,1)S(1)}, bf16[8,1024]{1,0:T(8,128)(2,1)}, u32[]{:S(2)}) copy-start(bf16[8,1024]{1,0:T(8,128)(2,1)} %param.14) | copy-start | bytes 49156
  208.2 50.9 %copy-start.3 = (bf16[8,128]{1,0:T(8,128)(2,1)S(1)}, bf16[8,128]{1,0:T(8,128)(2,1)}, u32[]{:S(2)}) copy-start(bf16[8,128]{1,0:T(8,128)(2,1)} %param.16) | copy-start | bytes 6148
  213.1 18.8 %collective-permute-start.25 = (bf16[128,128]{1,0:T(8,128)(2,1)S(1)}, bf16[128,128]{1,0:T(8,128)(2,1)S(1)}, u32[]{:S(2)}, u32[]{:S(2)}) collective-permute-start(bf16[128,128]{1,0:T(8,128)(2,1)S(1)} %get-tuple-element.28), channel_id=1, source_target_pairs={{0,424},{8,432},{16,440},{24,448},{32,456},{40,464},{48,472},{56,4... | collective-permute-start | bytes 98312 | tf_op jit(solution)/shard_map/ppermute | solution.py:18
  217.6 19.6 %collective-permute-start.24 = (bf16[128,128]{1,0:T(8,128)(2,1)S(1)}, bf16[128,128]{1,0:T(8,128)(2,1)S(1)}, u32[]{:S(2)}, u32[]{:S(2)}) collective-permute-start(bf16[128,128]{1,0:T(8,128)(2,1)S(1)} %get-tuple-element.29), channel_id=1, source_target_pairs={{0,432},{8,440},{16,448},{24,456},{32,464},{40,472},{48,480},{56,4... | collective-permute-start | bytes 98312 | tf_op jit(solution)/shard_map/ppermute | solution.py:18
  219.6 23.9 %collective-permute-start.23 = (bf16[128,128]{1,0:T(8,128)(2,1)S(1)}, bf16[128,128]{1,0:T(8,128)(2,1)S(1)}, u32[]{:S(2)}, u32[]{:S(2)}) collective-permute-start(bf16[128,128]{1,0:T(8,128)(2,1)S(1)} %get-tuple-element.30), channel_id=1, source_target_pairs={{0,440},{8,448},{16,456},{24,464},{32,472},{40,480},{48,488},{56,4... | collective-permute-start | bytes 98312 | tf_op jit(solution)/shard_map/ppermute | solution.py:18
  224.6 22.1 %collective-permute-start.22 = (bf16[128,128]{1,0:T(8,128)(2,1)S(1)}, bf16[128,128]{1,0:T(8,128)(2,1)S(1)}, u32[]{:S(2)}, u32[]{:S(2)}) collective-permute-start(bf16[128,128]{1,0:T(8,128)(2,1)S(1)} %get-tuple-element.31), channel_id=1, source_target_pairs={{0,448},{8,456},{16,464},{24,472},{32,480},{40,488},{48,496},{56,5... | collective-permute-start | bytes 98312 | tf_op jit(solution)/shard_map/ppermute | solution.py:18
  228.8 21.5 %collective-permute-start.21 = (bf16[128,128]{1,0:T(8,128)(2,1)S(1)}, bf16[128,128]{1,0:T(8,128)(2,1)S(1)}, u32[]{:S(2)}, u32[]{:S(2)}) collective-permute-start(bf16[128,128]{1,0:T(8,128)(2,1)S(1)} %get-tuple-element.32), channel_id=1, source_target_pairs={{0,456},{8,464},{16,472},{24,480},{32,488},{40,496},{48,504},{56,0... | collective-permute-start | bytes 98312 | tf_op jit(solution)/shard_map/ppermute | solution.py:18
  231.9 22.3 %collective-permute-start.20 = (bf16[128,128]{1,0:T(8,128)(2,1)S(1)}, bf16[128,128]{1,0:T(8,128)(2,1)S(1)}, u32[]{:S(2)}, u32[]{:S(2)}) collective-permute-start(bf16[128,128]{1,0:T(8,128)(2,1)S(1)} %get-tuple-element.33), channel_id=1, source_target_pairs={{0,464},{8,472},{16,480},{24,488},{32,496},{40,504},{48,0},{56,8},... | collective-permute-start | bytes 98312 | tf_op jit(solution)/shard_map/ppermute | solution.py:18
  237.2 17.0 %collective-permute-start.19 = (bf16[128,128]{1,0:T(8,128)(2,1)S(1)}, bf16[128,128]{1,0:T(8,128)(2,1)S(1)}, u32[]{:S(2)}, u32[]{:S(2)}) collective-permute-start(bf16[128,128]{1,0:T(8,128)(2,1)S(1)} %get-tuple-element.34), channel_id=1, source_target_pairs={{0,472},{8,480},{16,488},{24,496},{32,504},{40,0},{48,8},{56,16},{... | collective-permute-start | bytes 98312 | tf_op jit(solution)/shard_map/ppermute | solution.py:18
  243.5 10.7 %collective-permute-start.18 = (bf16[128,128]{1,0:T(8,128)(2,1)S(1)}, bf16[128,128]{1,0:T(8,128)(2,1)S(1)}, u32[]{:S(2)}, u32[]{:S(2)}) collective-permute-start(bf16[128,128]{1,0:T(8,128)(2,1)S(1)} %get-tuple-element.35), channel_id=1, source_target_pairs={{0,480},{8,488},{16,496},{24,504},{32,0},{40,8},{48,16},{56,24},{6... | collective-permute-start | bytes 98312 | tf_op jit(solution)/shard_map/ppermute | solution.py:18
  246.7 8.8 %collective-permute-start.17 = (bf16[128,128]{1,0:T(8,128)(2,1)S(1)}, bf16[128,128]{1,0:T(8,128)(2,1)S(1)}, u32[]{:S(2)}, u32[]{:S(2)}) collective-permute-start(bf16[128,128]{1,0:T(8,128)(2,1)S(1)} %get-tuple-element.36), channel_id=1, source_target_pairs={{0,488},{8,496},{16,504},{24,0},{32,8},{40,16},{48,24},{56,32},{64... | collective-permute-start | bytes 98312 | tf_op jit(solution)/shard_map/ppermute | solution.py:18
  250.3 7.9 collective-permute-start.16
Sparse Core Ops, SparseCore 0:
  289.4 532.1 all-reduce.4
where the time goes:
time: 838 us; the launch traced here: 834 us
  waiting for transfers between devices  585 us (70%)
  starting transfers between devices  130 us (16%)
  blocking collectives  46.5 us (6%)
  matrix products  45.4 us (5%)
  between operations  14.7 us (2%)
  local copies, waits for them, and re-layouts  8.66 us (1%)
    psum x1, waiting for transfers between devices, per_device(): lax.psum((down_grad_query, grad_up_query, down_grad_value, grad_up_value)...  531 us
    ppermute x30, starting transfers between devices, shifted_2(): return lax.ppermute(value, axis, pairs)  130 us
    ppermute x30, waiting for transfers between devices, shifted_2(): return lax.ppermute(value, axis, pairs)  53.6 us
    psum x1, blocking collectives, per_device(): lax.psum((part_grad_query, part_grad_value), 'tensor')  28.3 us
    psum x1, blocking collectives, per_device(): low_query, low_value = lax.psum((part_query, part_value), 'tensor')  18.2 us
  transfers between devices with their start and end apart: 31, of which 14 were waited for; matrix products, arithmetic and copies ran while one was open for 2% of the time, Pallas kernels for 0%

commit v1 on v0

v1 whole, which is shorter than its diff:
```python
import functools
import math

import jax
import jax.numpy as jnp
from jax import lax
from jax.experimental import pallas as pl
from jax.experimental.pallas import tpu as pltpu
from jax.sharding import PartitionSpec as P

MESH = pl.DeviceIdType.MESH
GROUP_TOKENS = 2048
HEADS = 8
HEAD = 128
RANK = 8
TOK = 128
WIDTH = HEADS * HEAD
GAIN = 2.0
ROOT = HEAD ** -0.5
LOG2E = math.log2(math.e)
F32 = jnp.float32
BF16 = jnp.bfloat16
NT = (((1,), (1,)), ((), ()))


def dot(a, b):
    return jnp.dot(a, b, preferred_element_type=F32)


def dot_nt(a, b):
    return lax.dot_general(a, b, NT, preferred_element_type=F32)


def split2(x):
    hi = x.astype(BF16).astype(F32)
    return hi, x - hi


def kernel(
    n_seq, n_tensor, group,
    hid, qb, kp, fv, dq, uq, dv, uv, go,
    att, gdq, guq, gdv, guv,
    parts1, parts2, kbuf, vbuf, vown, lgout, lgin, ain, bin_, cin, aout,
    qs, sbuf, ebuf, dpbuf, stat, linv, oacc, dqacc, dol, dqhi, dqlo,
    p1s, p1r, ks, kf, kr, vs, vf, vr, ls, lr, p2s, p2r, asd, ard, bsd, brd, csd, crd,
):
    s = lax.axis_index("seq")
    t = lax.axis_index("tensor")
    chips = group // 2
    n_groups = n_seq // group
    wide = WIDTH // chips
    lag = jnp.where(t >= n_tensor // 2, group // 2, 0)
    rolled = lax.rem(s - lag + n_seq, n_seq)
    g = rolled // group
    p = lax.rem(rolled, group)
    c = p // 2
    yl = lax.rem(p, 2)
    mate = 2 * c + 1 - yl

    def place(gg, pp):
        return lax.rem(gg * group + pp + lag, n_seq)

    def dev(gg, pp):
        return (place(gg, pp), t)

    def remote(src, dst, send, recv, device):
        return pltpu.make_async_remote_copy(
            src_ref=src, dst_ref=dst, send_sem=send, recv_sem=recv,
            device_id=device, device_id_type=MESH,
        )

    barrier = pltpu.get_barrier_semaphore()

    def greet(device):
        pl.semaphore_signal(barrier, inc=1, device_id=device, device_id_type=MESH)

    def greet_tensor(i, carry):
        greet((s, lax.rem(t + i, n_tensor)))
        return carry

    def greet_group(i, carry):
        greet(dev(g, lax.rem(p + i, group)))
        return carry

    def greet_far(i, carry):
        greet(dev(lax.rem(g + 1 + i // 2, n_groups), 2 * c + lax.rem(i, 2)))
        return carry

    lax.fori_loop(1, n_tensor, greet_tensor, 0)
    lax.fori_loop(1, group, greet_group, 0)
    lax.fori_loop(0, 2 * (n_groups - 1), greet_far, 0)

    down = jnp.concatenate([dq[...].astype(F32), dv[...].astype(F32)], axis=0).astype(BF16)
    parts1[t] = dot_nt(down, hid[...])
    kbuf[p] = kp[...]

    pl.semaphore_wait(barrier, (n_tensor - 1) + (group - 1) + 2 * (n_groups - 1))

    def part1_copy(i):
        peer = lax.rem(t + i, n_tensor)
        return remote(parts1.at[t], parts1.at[t], p1s.at[i], p1r.at[t], (s, peer))

    def start_part1(i, carry):
        part1_copy(i).start()
        return carry

    lax.fori_loop(1, n_tensor, start_part1, 0)

    def k_copy(to):
        return remote(kp, kbuf.at[p], ks.at[to], kr.at[p], dev(g, 2 * to + yl))

    def k_pair(frm):
        return remote(kbuf.at[2 * frm + yl], kbuf.at[2 * frm + yl], kf.at[frm], kr.at[2 * frm + yl], dev(g, mate))

    def v_copy(to):
        return remote(vown, vbuf.at[p], vs.at[to], vr.at[p], dev(g, 2 * to + yl))

    def v_pair(frm):
        return remote(vbuf.at[2 * frm + yl], vbuf.at[2 * frm + yl], vf.at[frm], vr.at[2 * frm + yl], dev(g, mate))

    def k_wait(pp):
        pltpu.make_async_copy(kbuf.at[pp], kbuf.at[pp], kr.at[pp]).wait()

    def v_wait(pp):
        pltpu.make_async_copy(vbuf.at[pp], vbuf.at[pp], vr.at[pp]).wait()

    k_pair(c).start()

    def start_k(to, carry):
        k_copy(to).start()
        return carry

    lax.fori_loop(c + 1, chips, start_k, 0)

    def wait_part1(i, carry):
        src = lax.rem(t + i, n_tensor)
        pltpu.make_async_copy(parts1.at[src], parts1.at[src], p1r.at[src]).wait()
        return carry

    lax.fori_loop(1, n_tensor, wait_part1, 0)
    low = parts1[0]
    for i in range(1, n_tensor):
        low = low + parts1[i]
    hi = low.astype(BF16).astype(F32)
    rest = low - hi
    mid = rest.astype(BF16).astype(F32)
    lo = rest - mid
    zeros = jnp.zeros((TOK - 48, TOK), F32)
    pieces = jnp.transpose(jnp.concatenate([hi, mid, lo, zeros], axis=0)).astype(BF16)
    none_q = jnp.zeros((RANK, WIDTH), F32)
    none_v = jnp.zeros((RANK, HEAD), F32)
    uqf = uq[...].astype(F32)
    uvf = uv[...].astype(F32)
    up_v = jnp.concatenate([none_v, uvf] * 3 + [jnp.zeros((TOK - 48, HEAD), F32)], axis=0).astype(BF16)
    value = (fv[...].astype(F32) + GAIN * dot(pieces, up_v)).astype(BF16)
    low_v = jnp.concatenate([hi[RANK:], rest[RANK:]], axis=0).astype(BF16)
    vown[0:TOK, :] = value
    vown[TOK:TOK + 16, :] = low_v
    vbuf[p] = vown[...]

    v_pair(c).start()

    def start_v(to, carry):
        v_copy(to).start()
        return carry

    lax.fori_loop(c + 1, chips, start_v, 0)

    up_q = jnp.concatenate([uqf, none_q] * 3 + [jnp.zeros((TOK - 48, WIDTH), F32)], axis=0).astype(BF16)
    for h in range(HEADS):
        cols = slice(h * HEAD, (h + 1) * HEAD)
        qs[cols, :] = (qb[:, cols].astype(F32) + GAIN * dot(pieces, up_q[:, cols])).astype(BF16)

    def forward_k(i, carry):
        frm = c - 1 - i
        k_wait(2 * frm + yl)
        k_pair(frm).start()
        return carry

    def keys_of(ch):
        return kbuf[pl.ds(2 * ch, 2)].reshape(2 * TOK, HEAD)

    lax.fori_loop(0, c, forward_k, 0)
    k_wait(mate)
    kc = keys_of(c)
    column = lax.broadcasted_iota(jnp.int32, (TOK, 2 * TOK), 1)
    row = lax.broadcasted_iota(jnp.int32, (TOK, 2 * TOK), 0)
    allowed = column <= row + yl * TOK
    for h in range(HEADS):
        rows = slice(h * TOK, (h + 1) * TOK)
        sc = jnp.where(allowed, dot_nt(qs[rows, :], kc) * (ROOT * LOG2E), -1e30)
        sbuf[c, rows, :] = sc
        stat[rows, :] = jnp.maximum(sc[:, :TOK], sc[:, TOK:])

    def scores(i, carry):
        ch = c - 1 - i
        k_wait(2 * ch + 1 - yl)
        kc = keys_of(ch)
        for h in range(HEADS):
            rows = slice(h * TOK, (h + 1) * TOK)
            sc = dot_nt(qs[rows, :], kc) * (ROOT * LOG2E)
            sbuf[ch, rows, :] = sc
            stat[rows, :] = jnp.maximum(stat[rows, :], jnp.maximum(sc[:, :TOK], sc[:, TOK:]))
        return carry

    lax.fori_loop(0, c, scores, 0)
    for h in range(HEADS):
        rows = slice(h * TOK, (h + 1) * TOK)
        stat[rows, :] = jnp.broadcast_to(jnp.max(stat[rows, :], axis=1, keepdims=True), (TOK, HEAD))
    linv[...] = jnp.zeros_like(linv)

    def exps(i, carry):
        ch = c - i

        @pl.when(i > 0)
        def _():
            v_wait(2 * ch + yl)
            v_pair(ch).start()

        for h in range(HEADS):
            rows = slice(h * TOK, (h + 1) * TOK)
            m = stat[rows, :]
            e0 = jnp.exp2(sbuf[ch, rows, 0:TOK] - m)
            e1 = jnp.exp2(sbuf[ch, rows, TOK:2 * TOK] - m)
            linv[rows, :] += e0 + e1
            ebuf[ch, rows, 0:TOK] = e0.astype(BF16)
            ebuf[ch, rows, TOK:2 * TOK] = e1.astype(BF16)
        return carry

    lax.fori_loop(0, c + 1, exps, 0)
    for h in range(HEADS):
        rows = slice(h * TOK, (h + 1) * TOK)
        inv = 1.0 / jnp.sum(linv[rows, :], axis=1, keepdims=True)
        linv[rows, :] = jnp.broadcast_to(inv, (TOK, HEAD))
        dol[rows, :] = (go[:, rows].astype(F32) * inv).astype(BF16)

    weights = dot_nt(uv[...], dol[...])
    w_hi, w_lo = split2(weights)
    w16 = jnp.concatenate([w_hi, w_lo], axis=0).astype(BF16)

    def lg_copy(to):
        return remote(lgout.at[to], lgin.at[p], ls.at[to], lr.at[p], dev(g, to))

    def grads(i, carry):
        ch = c - i
        both = dot(w16, ebuf[ch])
        lg = GAIN * (both[0:RANK] + both[RANK:2 * RANK])
        lgout[2 * ch] = lg[:, 0:TOK]
        lgout[2 * ch + 1] = lg[:, TOK:2 * TOK]

        @pl.when(2 * ch < p)
        def _():
            lg_copy(2 * ch).start()

        @pl.when(2 * ch + 1 < p)
        def _():
            lg_copy(2 * ch + 1).start()

        return carry

    lax.fori_loop(0, c + 1, grads, 0)

    oacc[...] = jnp.zeros_like(oacc)
    dqacc[...] = jnp.zeros_like(dqacc)

    def outs(i, tt):
        ch = c - i
        v_wait(2 * ch + 1 - yl)
        vc = jnp.concatenate([vbuf[2 * ch, 0:TOK, :], vbuf[2 * ch + 1, 0:TOK, :]], axis=0)
        lows = jnp.concatenate([vbuf[2 * ch, TOK:TOK + 16, :], vbuf[2 * ch + 1, TOK:TOK + 16, :]], axis=1)
        for h in range(HEADS):
            rows = slice(h * TOK, (h + 1) * TOK)
            oacc[rows, :] += dot(ebuf[ch, rows, :], vc)
            dpbuf[ch, rows, :] = dot_nt(go[:, rows], vc)
        return tt + dot_nt(lows, ebuf[ch])

    tt = lax.fori_loop(0, c + 1, outs, jnp.zeros((16, HEADS * TOK), F32))
    for h in range(HEADS):
        rows = slice(h * TOK, (h + 1) * TOK)
        o = oacc[rows, :] * linv[rows, :]
        att[:, rows] = o.astype(BF16)
        center = jnp.sum(o * go[:, rows].astype(F32), axis=1, keepdims=True)
        stat[rows, :] = jnp.broadcast_to(center, (TOK, HEAD))

    def dquery(i, carry):
        ch = c - i
        kc = keys_of(ch)
        for h in range(HEADS):
            rows = slice(h * TOK, (h + 1) * TOK)
            cen = stat[rows, :]
            d0 = ebuf[ch, rows, 0:TOK].astype(F32) * (dpbuf[ch, rows, 0:TOK] - cen)
            d1 = ebuf[ch, rows, TOK:2 * TOK].astype(F32) * (dpbuf[ch, rows, TOK:2 * TOK] - cen)
            dqacc[rows, :] += dot(jnp.concatenate([d0.astype(BF16), d1.astype(BF16)], axis=1), kc)
        return carry

    lax.fori_loop(0, c + 1, dquery, 0)
    for h in range(HEADS):
        rows = slice(h * TOK, (h + 1) * TOK)
        d_hi, d_lo = split2(dqacc[rows, :] * (linv[rows, :] * ROOT))
        dqhi[:, rows] = d_hi.astype(BF16)
        dqlo[:, rows] = d_lo.astype(BF16)
    lgq = GAIN * (dot_nt(uq[...], dqhi[...]) + dot_nt(uq[...], dqlo[...]))

    def wait_lg(pp, acc):
        pltpu.make_async_copy(lgin.at[pp], lgin.at[pp], lr.at[pp]).wait()
        return acc + lgin[pp]

    lgv = lax.fori_loop(p + 1, group, wait_lg, lgout[p])
    parts2[t] = jnp.concatenate([lgq, lgv], axis=0)

    def part2_copy(i):
        peer = lax.rem(t + i, n_tensor)
        return remote(parts2.at[t], parts2.at[t], p2s.at[i], p2r.at[t], (s, peer))

    def start_part2(i, carry):
        part2_copy(i).start()
        return carry

    lax.fori_loop(1, n_tensor, start_part2, 0)

    lq16 = jnp.concatenate([hi[:RANK], rest[:RANK]], axis=0).astype(BF16)
    g_up = dot(lq16, dqhi[...])
    g_lo = dot(lq16, dqlo[...])
    g_up_q = GAIN * (g_up[:RANK] + g_up[RANK:] + g_lo[:RANK])
    t_hi, t_lo = split2(tt[:RANK] + tt[RANK:])
    g_v = dot(jnp.concatenate([t_hi, t_lo], axis=0).astype(BF16), dol[...])
    g_up_v = GAIN * (g_v[:RANK] + g_v[RANK:])
    rank_row = lax.broadcasted_iota(jnp.int32, (RANK, HEAD), 0)
    for k in range(chips):
        aout[k, RANK:2 * RANK, :] = g_up_q[:, k * wide:(k + 1) * wide]
        if wide > HEAD:
            aout[k, 3 * RANK:4 * RANK, :] = jnp.zeros((RANK, wide), F32)
        aout[k, 3 * RANK:4 * RANK, 0:HEAD] = jnp.where(lax.rem(rank_row, chips) == k, g_up_v, 0.0)

    def wait_part2(i, carry):
        src = lax.rem(t + i, n_tensor)
        pltpu.make_async_copy(parts2.at[src], parts2.at[src], p2r.at[src]).wait()
        return carry

    lax.fori_loop(1, n_tensor, wait_part2, 0)
    lowg = parts2[0]
    for i in range(1, n_tensor):
        lowg = lowg + parts2[i]
    g_down = dot(lowg.astype(BF16), hid[...])
    for k in range(chips):
        aout[k, 0:RANK, :] = g_down[0:RANK, k * wide:(k + 1) * wide]
        aout[k, 2 * RANK:3 * RANK, :] = g_down[RANK:2 * RANK, k * wide:(k + 1) * wide]

    def a_copy(i):
        to = lax.rem(c + i, chips)
        return remote(aout.at[to], ain.at[c], asd.at[i], ard.at[c], dev(g, 2 * to + yl))

    def c_copy(i):
        to = lax.rem(c + i, chips)
        return remote(cin.at[c], cin.at[c], csd.at[i], crd.at[c], dev(g, 2 * to + yl))

    mine = 2 * g + yl

    def b_copy(i):
        slot = lax.rem(mine + i, 2 * n_groups)
        return remote(
            bin_.at[mine], bin_.at[mine], bsd.at[i], brd.at[mine],
            dev(slot // 2, 2 * c + lax.rem(slot, 2)),
        )

    def start_a(i, carry):
        a_copy(i).start()
        return carry

    def start_b(i, carry):
        b_copy(i).start()
        return carry

    def start_c(i, carry):
        c_copy(i).start()
        return carry

    def waiter(buf, sem, me, count):
        def body(i, carry):
            src = lax.rem(me + i, count)
            pltpu.make_async_copy(buf.at[src], buf.at[src], sem.at[src]).wait()
            return carry

        lax.fori_loop(1, count, body, 0)

    lax.fori_loop(1, chips, start_a, 0)
    ain[c] = aout[c]
    waiter(ain, ard, c, chips)
    total = ain[0]
    for k in range(1, chips):
        total = total + ain[k]
    bin_[mine] = total
    lax.fori_loop(1, 2 * n_groups, start_b, 0)
    waiter(bin_, brd, mine, 2 * n_groups)
    total = bin_[0]
    for k in range(1, 2 * n_groups):
        total = total + bin_[k]
    cin[c] = total
    lax.fori_loop(1, chips, start_c, 0)
    waiter(cin, crd, c, chips)
    up_total = jnp.zeros((RANK, HEAD), F32)
    for k in range(chips):
        gdq[:, k * wide:(k + 1) * wide] = cin[k, 0:RANK, :]
        guq[:, k * wide:(k + 1) * wide] = cin[k, RANK:2 * RANK, :]
        gdv[:, k * wide:(k + 1) * wide] = cin[k, 2 * RANK:3 * RANK, :]
        up_total = up_total + cin[k, 3 * RANK:4 * RANK, 0:HEAD]
    guv[...] = up_total

    def end_tensor(i, carry):
        part1_copy(i).wait_send()
        part2_copy(i).wait_send()
        return carry

    def end_later(to, carry):
        k_copy(to).wait_send()
        v_copy(to).wait_send()
        return carry

    def end_pair(frm, carry):
        k_pair(frm).wait_send()
        v_pair(frm).wait_send()
        return carry

    def end_lg(to, carry):
        lg_copy(to).wait_send()
        return carry

    def end_row(i, carry):
        a_copy(i).wait_send()
        c_copy(i).wait_send()
        return carry

    def end_far(i, carry):
        b_copy(i).wait_send()
        return carry

    lax.fori_loop(1, n_tensor, end_tensor, 0)
    lax.fori_loop(c + 1, chips, end_later, 0)
    lax.fori_loop(0, c + 1, end_pair, 0)
    lax.fori_loop(0, p, end_lg, 0)
    lax.fori_loop(1, chips, end_row, 0)
    lax.fori_loop(1, 2 * n_groups, end_far, 0)


def solution(mesh, group_tokens=GROUP_TOKENS):
    n_seq, n_tensor = mesh.shape["seq"], mesh.shape["tensor"]
    group = group_tokens // TOK
    chips = group // 2
    far = 2 * (n_seq // group)
    wide = WIDTH // chips
    rows = HEADS * TOK
    vmem = pl.BlockSpec(memory_space=pltpu.VMEM)
    dma = pltpu.SemaphoreType.DMA

    def per_device(*args):
        return pl.pallas_call(
            functools.partial(kernel, n_seq, n_tensor, group),
            out_shape=(
                jax.ShapeDtypeStruct((TOK, WIDTH), BF16),
                jax.ShapeDtypeStruct((RANK, WIDTH), F32),
                jax.ShapeDtypeStruct((RANK, WIDTH), F32),
                jax.ShapeDtypeStruct((RANK, WIDTH), F32),
                jax.ShapeDtypeStruct((RANK, HEAD), F32),
            ),
            in_specs=[vmem] * 9,
            out_specs=(vmem,) * 5,
            scratch_shapes=[
                pltpu.VMEM((n_tensor, 2 * RANK, TOK), F32),
                pltpu.VMEM((n_tensor, 2 * RANK, TOK), F32),
                pltpu.VMEM((group, TOK, HEAD), BF16),
                pltpu.VMEM((group, TOK + 16, HEAD), BF16),
                pltpu.VMEM((TOK + 16, HEAD), BF16),
                pltpu.VMEM((group, RANK, TOK), F32),
                pltpu.VMEM((group, RANK, TOK), F32),
                pltpu.VMEM((chips, 4 * RANK, wide), F32),
                pltpu.VMEM((far, 4 * RANK, wide), F32),
                pltpu.VMEM((chips, 4 * RANK, wide), F32),
                pltpu.VMEM((chips, 4 * RANK, wide), F32),
                pltpu.VMEM((rows, HEAD), BF16),
                pltpu.VMEM((chips, rows, 2 * TOK), F32),
                pltpu.VMEM((chips, rows, 2 * TOK), BF16),
                pltpu.VMEM((chips, rows, 2 * TOK), F32),
                pltpu.VMEM((rows, HEAD), F32),
                pltpu.VMEM((rows, HEAD), F32),
                pltpu.VMEM((rows, HEAD), F32),
                pltpu.VMEM((rows, HEAD), F32),
                pltpu.VMEM((rows, HEAD), BF16),
                pltpu.VMEM((TOK, WIDTH), BF16),
                pltpu.VMEM((TOK, WIDTH), BF16),
                dma((n_tensor,)), dma((n_tensor,)),
                dma((chips,)), dma((chips,)), dma((group,)),
                dma((chips,)), dma((chips,)), dma((group,)),
                dma((group,)), dma((group,)),
                dma((n_tensor,)), dma((n_tensor,)),
                dma((chips,)), dma((chips,)),
                dma((far,)), dma((far,)),
                dma((chips,)), dma((chips,)),
            ],
            compiler_params=pltpu.CompilerParams(
                collective_id=0, has_side_effects=True, vmem_limit_bytes=48 * 1024 * 1024
            ),
        )(*args)

    split = P("seq", "tensor")
    cols = P(None, "tensor")
    return jax.shard_map(
        per_device,
        mesh=mesh,
        in_specs=(split, split, split, split, cols, cols, cols, cols, split),
        out_specs=(split, cols, cols, cols, cols),
        check_vma=False,
    )
```

time: 838 us -> 70.8 us (0.08)
  waiting for transfers between devices: 585 us -> 0 us
  starting transfers between devices: 130 us -> 0 us
  Pallas kernels: 0 us -> 58.9 us
  blocking collectives: 46.5 us -> 0 us
  matrix products: 45.4 us -> 0 us
  between operations: 14.7 us -> 0.66 us
    psum x1 -> x0, waiting for transfers between devices: 531 us -> none  [per_device(): lax.psum((down_grad_query, grad_up_query, down_grad_value, grad_up_value)...]
    ppermute x30 -> x0, starting transfers between devices: 130 us -> none  [shifted_2(): return lax.ppermute(value, axis, pairs)]
    pallas_call x0 -> x1, Pallas kernels: none -> 58.9 us  [per_device(): pl.pallas_call(functools.partial(kernel, n_seq, n_tensor, group), out_sha...]
    ppermute x30 -> x0, waiting for transfers between devices: 53.6 us -> none  [shifted_2(): return lax.ppermute(value, axis, pairs)]
    psum x2 -> x0, blocking collectives: 46.5 us -> none  [the longest x1 28.3 us: per_device(): lax.psum((part_grad_query, part_grad_value), 'tensor')]
    dot_general x18 -> x0, matrix products: 38.8 us -> none  [the longest x2 9.73 us: per_device(): jnp.einsum('thd,cd->htc', cot_part, value_head, preferred_element_type=jn...]
  transfers between devices with their start and end apart: 31 -> 0, of which waited for: 14 -> 0; matrix products, arithmetic and copies ran while one was open for 2% -> 0% of each run, Pallas kernels for 0% -> 0%
where the time goes in v1:
time: 70.8 us; the launch traced here: 69.9 us
  Pallas kernels  58.9 us (83%)
  local copies, waits for them, and re-layouts  10.3 us (15%)
    pallas_call x1, Pallas kernels, per_device(): pl.pallas_call(functools.partial(kernel, n_seq, n_tensor, group), out_sha...  58.9 us
    unnamed x23, local copies, waits for them, and re-layouts  10.3 us

profile of v1, /device:TPU:6, one launch (start us, length us, event | category | flops | bytes accessed | tf_op | source)
XLA Modules:
  0.0 69.9 jit_solution(14271087846952694121)
XLA Ops:
  0.6 0.0 copy-start
  0.6 0.9 %copy-done = bf16[128,1024]{1,0:T(8,128)(2,1)S(1)} copy-done((bf16[128,1024]{1,0:T(8,128)(2,1)S(1)}, bf16[128,1024]{1,0:T(8,128)(2,1)}, u32[]{:S(2)}) %copy-start) | copy-done | bytes 262168
  1.6 0.0 copy-start.1
  1.6 0.9 %copy-done.1 = bf16[128,1024]{1,0:T(8,128)(2,1)S(1)} copy-done((bf16[128,1024]{1,0:T(8,128)(2,1)S(1)}, bf16[128,1024]{1,0:T(8,128)(2,1)}, u32[]{:S(2)}) %copy-start.1) | copy-done | bytes 262168
  2.5 0.0 copy-start.2
  2.5 0.9 %copy-done.2 = bf16[128,1024]{1,0:T(8,128)(2,1)S(1)} copy-done((bf16[128,1024]{1,0:T(8,128)(2,1)S(1)}, bf16[128,1024]{1,0:T(8,128)(2,1)}, u32[]{:S(2)}) %copy-start.2) | copy-done | bytes 262168
  3.5 0.0 copy-start.3
  3.5 0.8 %copy-done.3 = bf16[128,128]{1,0:T(8,128)(2,1)S(1)} copy-done((bf16[128,128]{1,0:T(8,128)(2,1)S(1)}, bf16[128,128]{1,0:T(8,128)(2,1)}, u32[]{:S(2)}) %copy-start.3) | copy-done | bytes 32792
  4.2 0.0 copy-start.4
  4.2 0.8 %copy-done.4 = bf16[128,128]{1,0:T(8,128)(2,1)S(1)} copy-done((bf16[128,128]{1,0:T(8,128)(2,1)S(1)}, bf16[128,128]{1,0:T(8,128)(2,1)}, u32[]{:S(2)}) %copy-start.4) | copy-done | bytes 32792
  5.0 0.0 copy-start.5
  5.0 0.7 %copy-done.5 = bf16[8,1024]{1,0:T(8,128)(2,1)S(1)} copy-done((bf16[8,1024]{1,0:T(8,128)(2,1)S(1)}, bf16[8,1024]{1,0:T(8,128)(2,1)}, u32[]{:S(2)}) %copy-start.5) | copy-done | bytes 16408
  5.7 0.0 copy-start.6
  5.7 0.7 %copy-done.6 = bf16[8,1024]{1,0:T(8,128)(2,1)S(1)} copy-done((bf16[8,1024]{1,0:T(8,128)(2,1)S(1)}, bf16[8,1024]{1,0:T(8,128)(2,1)}, u32[]{:S(2)}) %copy-start.6) | copy-done | bytes 16408
  6.4 0.0 copy-start.7
  6.4 0.7 %copy-done.7 = bf16[8,1024]{1,0:T(8,128)(2,1)S(1)} copy-done((bf16[8,1024]{1,0:T(8,128)(2,1)S(1)}, bf16[8,1024]{1,0:T(8,128)(2,1)}, u32[]{:S(2)}) %copy-start.7) | copy-done | bytes 16408
  7.2 0.0 copy-start.8
  7.2 0.7 copy-done.8
  7.8 58.9 %shard_map.128 = (bf16[128,1024]{1,0:T(8,128)(2,1)S(1)}, f32[8,1024]{1,0:T(8,128)S(1)}, f32[8,1024]{1,0:T(8,128)S(1)}, f32[8,1024]{1,0:T(8,128)S(1)}, f32[8,128]{1,0:T(8,128)S(1)}) custom-call(bf16[128,1024]{1,0:T(8,128)(2,1)S(1)} %copy-done, bf16[128,1024]{1,0:T(8,128)(2,1)S(1)} %copy-done.1, bf16[128,128]{1,0:T(8,128)(2,1)S(1)} %copy-done.3, ...), custom_call_target="tpu_custom_call" | custom-call | tf_op jit(solution)/shard_map/pallas_call | solution.py:456
  66.8 0.7 %copy.19 = bf16[128,1024]{1,0:T(8,128)(2,1)} copy(bf16[128,1024]{1,0:T(8,128)(2,1)S(1)} %get-tuple-element.10) | data formatting | bytes 524288
  67.5 0.6 copy.20
  68.1 0.6 copy.21
  68.7 0.6 copy.22
  69.3 0.6 copy.23
Async XLA Ops:
  0.6 1.0 %copy-start = (bf16[128,1024]{1,0:T(8,128)(2,1)S(1)}, bf16[128,1024]{1,0:T(8,128)(2,1)}, u32[]{:S(2)}) copy-start(bf16[128,1024]{1,0:T(8,128)(2,1)} %hid.1) | copy-start | bytes 786436
  1.6 0.9 %copy-start.1 = (bf16[128,1024]{1,0:T(8,128)(2,1)S(1)}, bf16[128,1024]{1,0:T(8,128)(2,1)}, u32[]{:S(2)}) copy-start(bf16[128,1024]{1,0:T(8,128)(2,1)} %qb.1) | copy-start | bytes 786436
  2.5 0.9 %copy-start.2 = (bf16[128,1024]{1,0:T(8,128)(2,1)S(1)}, bf16[128,1024]{1,0:T(8,128)(2,1)}, u32[]{:S(2)}) copy-start(bf16[128,1024]{1,0:T(8,128)(2,1)} %go.1) | copy-start | bytes 786436
  3.5 0.8 %copy-start.3 = (bf16[128,128]{1,0:T(8,128)(2,1)S(1)}, bf16[128,128]{1,0:T(8,128)(2,1)}, u32[]{:S(2)}) copy-start(bf16[128,128]{1,0:T(8,128)(2,1)} %kp.1) | copy-start | bytes 98308
  4.2 0.8 %copy-start.4 = (bf16[128,128]{1,0:T(8,128)(2,1)S(1)}, bf16[128,128]{1,0:T(8,128)(2,1)}, u32[]{:S(2)}) copy-start(bf16[128,128]{1,0:T(8,128)(2,1)} %fv.1) | copy-start | bytes 98308
  5.0 0.7 %copy-start.5 = (bf16[8,1024]{1,0:T(8,128)(2,1)S(1)}, bf16[8,1024]{1,0:T(8,128)(2,1)}, u32[]{:S(2)}) copy-start(bf16[8,1024]{1,0:T(8,128)(2,1)} %dq.1) | copy-start | bytes 49156
  5.7 0.7 %copy-start.6 = (bf16[8,1024]{1,0:T(8,128)(2,1)S(1)}, bf16[8,1024]{1,0:T(8,128)(2,1)}, u32[]{:S(2)}) copy-start(bf16[8,1024]{1,0:T(8,128)(2,1)} %uq.1) | copy-start | bytes 49156
  6.4 0.7 %copy-start.7 = (bf16[8,1024]{1,0:T(8,128)(2,1)S(1)}, bf16[8,1024]{1,0:T(8,128)(2,1)}, u32[]{:S(2)}) copy-start(bf16[8,1024]{1,0:T(8,128)(2,1)} %dv.1) | copy-start | bytes 49156
  7.2 0.7 copy-start.8

commit v2 on v1

--- a/solution.py
+++ b/solution.py
@@ -36,10 +36,16 @@
     return hi, x - hi
 
 
+def arrived(buf, sem):
+    pltpu.make_async_copy(buf, buf, sem).wait()
+
+
 def kernel(
     n_seq, n_tensor, group,
-    hid, qb, kp, fv, dq, uq, dv, uv, go,
-    att, gdq, guq, gdv, guv,
+    hid_h, qb_h, kp_h, fv_h, dq_h, uq_h, dv_h, uv_h, go_h,
+    att_h, gdq_h, guq_h, gdv_h, guv_h,
+    att, gdq, guq, gdv, guv, unload,
+    hid, qb, kp, fv, dq, uq, dv, uv, go, load,
     parts1, parts2, kbuf, vbuf, vown, lgout, lgin, ain, bin_, cin, aout,
     qs, sbuf, ebuf, dpbuf, stat, linv, oacc, dqacc, dol, dqhi, dqlo,
     p1s, p1r, ks, kf, kr, vs, vf, vr, ls, lr, p2s, p2r, asd, ard, bsd, brd, csd, crd,
@@ -69,6 +75,15 @@
             device_id=device, device_id_type=MESH,
         )
 
+    loads = [
+        pltpu.make_async_copy(src, dst, load.at[i])
+        for i, (src, dst) in enumerate((
+            (hid_h, hid), (dq_h, dq), (dv_h, dv), (kp_h, kp), (fv_h, fv), (uv_h, uv), (uq_h, uq), (qb_h, qb), (go_h, go),
+        ))
+    ]
+    for copy in loads[:4]:
+        copy.start()
+
     barrier = pltpu.get_barrier_semaphore()
 
     def greet(device):
@@ -90,6 +105,11 @@
     lax.fori_loop(1, group, greet_group, 0)
     lax.fori_loop(0, 2 * (n_groups - 1), greet_far, 0)
 
+    for copy in loads[4:]:
+        copy.start()
+    for copy in loads[:4]:
+        copy.wait()
+
     down = jnp.concatenate([dq[...].astype(F32), dv[...].astype(F32)], axis=0).astype(BF16)
     parts1[t] = dot_nt(down, hid[...])
     kbuf[p] = kp[...]
@@ -119,22 +139,33 @@
         return remote(vbuf.at[2 * frm + yl], vbuf.at[2 * frm + yl], vf.at[frm], vr.at[2 * frm + yl], dev(g, mate))
 
     def k_wait(pp):
-        pltpu.make_async_copy(kbuf.at[pp], kbuf.at[pp], kr.at[pp]).wait()
+        arrived(kbuf.at[pp], kr.at[pp])
 
     def v_wait(pp):
-        pltpu.make_async_copy(vbuf.at[pp], vbuf.at[pp], vr.at[pp]).wait()
+        arrived(vbuf.at[pp], vr.at[pp])
 
     k_pair(c).start()
 
     def start_k(to, carry):
-        k_copy(to).start()
-        return carry
-
-    lax.fori_loop(c + 1, chips, start_k, 0)
+        k_copy(chips - 1 - to).start()
+        return carry
+
+    lax.fori_loop(0, chips - 1 - c, start_k, 0)
+
+    for copy in loads[4:]:
+        copy.wait()
+
+    def forward_k(i, carry):
+        frm = c - 1 - i
+        k_wait(2 * frm + yl)
+        k_pair(frm).start()
+        return carry
+
+    lax.fori_loop(0, c, forward_k, 0)
 
     def wait_part1(i, carry):
         src = lax.rem(t + i, n_tensor)
-        pltpu.make_async_copy(parts1.at[src], parts1.at[src], p1r.at[src]).wait()
+        arrived(parts1.at[src], p1r.at[src])
         return carry
 
     lax.fori_loop(1, n_tensor, wait_part1, 0)
@@ -161,26 +192,19 @@
     v_pair(c).start()
 
     def start_v(to, carry):
-        v_copy(to).start()
-        return carry
-
-    lax.fori_loop(c + 1, chips, start_v, 0)
+        v_copy(chips - 1 - to).start()
+        return carry
+
+    lax.fori_loop(0, chips - 1 - c, start_v, 0)
 
     up_q = jnp.concatenate([uqf, none_q] * 3 + [jnp.zeros((TOK - 48, WIDTH), F32)], axis=0).astype(BF16)
     for h in range(HEADS):
         cols = slice(h * HEAD, (h + 1) * HEAD)
         qs[cols, :] = (qb[:, cols].astype(F32) + GAIN * dot(pieces, up_q[:, cols])).astype(BF16)
 
-    def forward_k(i, carry):
-        frm = c - 1 - i
-        k_wait(2 * frm + yl)
-        k_pair(frm).start()
-        return carry
-
     def keys_of(ch):
         return kbuf[pl.ds(2 * ch, 2)].reshape(2 * TOK, HEAD)
 
-    lax.fori_loop(0, c, forward_k, 0)
     k_wait(mate)
     kc = keys_of(c)
     column = lax.broadcasted_iota(jnp.int32, (TOK, 2 * TOK), 1)
@@ -263,24 +287,29 @@
     oacc[...] = jnp.zeros_like(oacc)
     dqacc[...] = jnp.zeros_like(dqacc)
 
-    def outs(i, tt):
+    def outs(i, carry):
         ch = c - i
         v_wait(2 * ch + 1 - yl)
         vc = jnp.concatenate([vbuf[2 * ch, 0:TOK, :], vbuf[2 * ch + 1, 0:TOK, :]], axis=0)
-        lows = jnp.concatenate([vbuf[2 * ch, TOK:TOK + 16, :], vbuf[2 * ch + 1, TOK:TOK + 16, :]], axis=1)
         for h in range(HEADS):
             rows = slice(h * TOK, (h + 1) * TOK)
             oacc[rows, :] += dot(ebuf[ch, rows, :], vc)
             dpbuf[ch, rows, :] = dot_nt(go[:, rows], vc)
-        return tt + dot_nt(lows, ebuf[ch])
-
-    tt = lax.fori_loop(0, c + 1, outs, jnp.zeros((16, HEADS * TOK), F32))
+        return carry
+
+    lax.fori_loop(0, c + 1, outs, 0)
     for h in range(HEADS):
         rows = slice(h * TOK, (h + 1) * TOK)
         o = oacc[rows, :] * linv[rows, :]
         att[:, rows] = o.astype(BF16)
         center = jnp.sum(o * go[:, rows].astype(F32), axis=1, keepdims=True)
         stat[rows, :] = jnp.broadcast_to(center, (TOK, HEAD))
+
+    unloads = [
+        pltpu.make_async_copy(src, dst, unload.at[i])
+        for i, (src, dst) in enumerate(((att, att_h), (gdq, gdq_h), (guq, guq_h), (gdv, gdv_h), (guv, guv_h)))
+    ]
+    unloads[0].start()
 
     def dquery(i, carry):
         ch = c - i
@@ -302,7 +331,7 @@
     lgq = GAIN * (dot_nt(uq[...], dqhi[...]) + dot_nt(uq[...], dqlo[...]))
 
     def wait_lg(pp, acc):
-        pltpu.make_async_copy(lgin.at[pp], lgin.at[pp], lr.at[pp]).wait()
+        arrived(lgin.at[pp], lr.at[pp])
         return acc + lgin[pp]
 
     lgv = lax.fori_loop(p + 1, group, wait_lg, lgout[p])
@@ -322,6 +351,12 @@
     g_up = dot(lq16, dqhi[...])
     g_lo = dot(lq16, dqlo[...])
     g_up_q = GAIN * (g_up[:RANK] + g_up[RANK:] + g_lo[:RANK])
+    def lows(i, tt):
+        ch = c - i
+        low16 = jnp.concatenate([vbuf[2 * ch, TOK:TOK + 16, :], vbuf[2 * ch + 1, TOK:TOK + 16, :]], axis=1)
+        return tt + dot_nt(low16, ebuf[ch])
+
+    tt = lax.fori_loop(0, c + 1, lows, jnp.zeros((16, HEADS * TOK), F32))
     t_hi, t_lo = split2(tt[:RANK] + tt[RANK:])
     g_v = dot(jnp.concatenate([t_hi, t_lo], axis=0).astype(BF16), dol[...])
     g_up_v = GAIN * (g_v[:RANK] + g_v[RANK:])
@@ -334,7 +369,7 @@
 
     def wait_part2(i, carry):
         src = lax.rem(t + i, n_tensor)
-        pltpu.make_async_copy(parts2.at[src], parts2.at[src], p2r.at[src]).wait()
+        arrived(parts2.at[src], p2r.at[src])
         return carry
 
     lax.fori_loop(1, n_tensor, wait_part2, 0)
@@ -378,7 +413,7 @@
     def waiter(buf, sem, me, count):
         def body(i, carry):
             src = lax.rem(me + i, count)
-            pltpu.make_async_copy(buf.at[src], buf.at[src], sem.at[src]).wait()
+            arrived(buf.at[src], sem.at[src])
             return carry
 
         lax.fori_loop(1, count, body, 0)
@@ -405,6 +440,8 @@
         gdv[:, k * wide:(k + 1) * wide] = cin[k, 2 * RANK:3 * RANK, :]
         up_total = up_total + cin[k, 3 * RANK:4 * RANK, 0:HEAD]
     guv[...] = up_total
+    for copy in unloads[1:]:
+        copy.start()
 
     def end_tensor(i, carry):
         part1_copy(i).wait_send()
@@ -440,6 +477,21 @@
     lax.fori_loop(0, p, end_lg, 0)
     lax.fori_loop(1, chips, end_row, 0)
     lax.fori_loop(1, 2 * n_groups, end_far, 0)
+    for copy in unloads:
+        copy.wait()
+
+
+def store(*refs):
+    made, out, held, sem = refs[0:5], refs[5:10], refs[10:15], refs[15]
+    copies = [pltpu.make_async_copy(made[i], held[i], sem.at[0, i]) for i in range(5)]
+    backs = [pltpu.make_async_copy(held[i], out[i], sem.at[1, i]) for i in range(5)]
+    for copy in copies:
+        copy.start()
+    for copy, back in zip(copies, backs):
+        copy.wait()
+        back.start()
+    for back in backs:
+        back.wait()
 
 
 def solution(mesh, group_tokens=GROUP_TOKENS):
@@ -449,22 +501,26 @@
     far = 2 * (n_seq // group)
     wide = WIDTH // chips
     rows = HEADS * TOK
-    vmem = pl.BlockSpec(memory_space=pltpu.VMEM)
     dma = pltpu.SemaphoreType.DMA
 
+    hbm = pl.BlockSpec(memory_space=pltpu.HBM)
+    results = (
+        jax.ShapeDtypeStruct((TOK, WIDTH), BF16),
+        jax.ShapeDtypeStruct((RANK, WIDTH), F32),
+        jax.ShapeDtypeStruct((RANK, WIDTH), F32),
+        jax.ShapeDtypeStruct((RANK, WIDTH), F32),
+        jax.ShapeDtypeStruct((RANK, HEAD), F32),
+    )
+
     def per_device(*args):
-        return pl.pallas_call(
+        made = pl.pallas_call(
             functools.partial(kernel, n_seq, n_tensor, group),
-            out_shape=(
-                jax.ShapeDtypeStruct((TOK, WIDTH), BF16),
-                jax.ShapeDtypeStruct((RANK, WIDTH), F32),
-                jax.ShapeDtypeStruct((RANK, WIDTH), F32),
-                jax.ShapeDtypeStruct((RANK, WIDTH), F32),
-                jax.ShapeDtypeStruct((RANK, HEAD), F32),
-            ),
-            in_specs=[vmem] * 9,
-            out_specs=(vmem,) * 5,
-            scratch_shapes=[
+            out_shape=results,
+            in_specs=[hbm] * 9,
+            out_specs=(hbm,) * 5,
+            scratch_shapes=[pltpu.VMEM(a.shape, a.dtype) for a in results] + [dma((5,))]
+            + [pltpu.VMEM(a.shape, a.dtype) for a in args] + [
+                dma((9,)),
                 pltpu.VMEM((n_tensor, 2 * RANK, TOK), F32),
                 pltpu.VMEM((n_tensor, 2 * RANK, TOK), F32),
                 pltpu.VMEM((group, TOK, HEAD), BF16),
@@ -497,9 +553,17 @@
                 dma((chips,)), dma((chips,)),
             ],
             compiler_params=pltpu.CompilerParams(
-                collective_id=0, has_side_effects=True, vmem_limit_bytes=48 * 1024 * 1024
+                collective_id=0, has_side_effects=True, vmem_limit_bytes=60 * 1024 * 1024
             ),
         )(*args)
+        return pl.pallas_call(
+            store,
+            out_shape=results,
+            in_specs=[hbm] * 5,
+            out_specs=(hbm,) * 5,
+            scratch_shapes=[pltpu.VMEM(a.shape, a.dtype) for a in results] + [dma((2, 5))],
+            compiler_params=pltpu.CompilerParams(vmem_limit_bytes=60 * 1024 * 1024),
+        )(*made)
 
     split = P("seq", "tensor")
     cols = P(None, "tensor")

time: 70.8 us -> 59.6 us (0.84)
  local copies, waits for them, and re-layouts: 10.3 us -> 0 us
    unnamed x23 -> x0, local copies, waits for them, and re-layouts: 10.3 us -> none
    pallas_call x1, Pallas kernels: 58.9 us -> 57 us  [per_device(): pl.pallas_call(functools.partial(kernel, n_seq, n_tensor, group), out_sha...]
    pallas_call x0 -> x1, Pallas kernels: none -> 1.76 us  [per_device(): pl.pallas_call(store, out_shape=results, in_specs=[hbm] * 5, out_specs=(h...]
where the time goes in v2:
time: 59.6 us; the launch traced here: 59.4 us
  Pallas kernels  58.8 us (99%)
  between operations  0.64 us (1%)
    pallas_call x1, Pallas kernels, per_device(): pl.pallas_call(functools.partial(kernel, n_seq, n_tensor, group), out_sha...  57 us
    pallas_call x1, Pallas kernels, per_device(): pl.pallas_call(store, out_shape=results, in_specs=[hbm] * 5, out_specs=(h...  1.76 us

profile of v2, /device:TPU:6, one launch (start us, length us, event | category | flops | bytes accessed | tf_op | source)
XLA Modules:
  0.0 59.4 jit_solution(12294082704821581355)
XLA Ops:
  0.6 57.0 %shard_map.128 = (bf16[128,1024]{1,0:T(8,128)(2,1)}, f32[8,1024]{1,0:T(8,128)}, f32[8,1024]{1,0:T(8,128)}, f32[8,1024]{1,0:T(8,128)}, f32[8,128]{1,0:T(8,128)}) custom-call(bf16[128,1024]{1,0:T(8,128)(2,1)} %hid_h.1, bf16[128,1024]{1,0:T(8,128)(2,1)} %qb_h.1, bf16[128,128]{1,0:T(8,128)(2,1)} %kp_h.1, bf16[128,128]{1,0:T(8,128)(2,1)} %fv_h.1, ...), custom_call_target="tpu_custom_call" | custom-call | tf_op jit(solution)/shard_map/pallas_call | solution.py:516
  57.6 1.8 %shard_map.129 = (bf16[128,1024]{1,0:T(8,128)(2,1)}, f32[8,1024]{1,0:T(8,128)}, f32[8,1024]{1,0:T(8,128)}, f32[8,1024]{1,0:T(8,128)}, f32[8,128]{1,0:T(8,128)}) custom-call(bf16[128,1024]{1,0:T(8,128)(2,1)} %get-tuple-element.10.refs_0_, f32[8,1024]{1,0:T(8,128)} %get-tuple-element.11.refs_1_, f32[8,1024]{1,0:T(8,128)} %get-tuple-element.12.refs_2_, ...), custom_call_target="tpu_custom_call" | custom-call | tf_op jit(solution)/shard_map/pallas_call | solution.py:559

commit v3 on v2

--- a/solution.py
+++ b/solution.py
@@ -21,6 +21,21 @@
 F32 = jnp.float32
 BF16 = jnp.bfloat16
 NT = (((1,), (1,)), ((), ()))
+
+
+def paced(count, body, width):
+    def step(i, carry):
+        for j in range(width):
+            body(i * width + j)
+        return carry
+
+    def rest(i, carry):
+        body(i)
+        return carry
+
+    whole = count // width
+    lax.fori_loop(0, whole, step, 0)
+    lax.fori_loop(whole * width, count, rest, 0)
 
 
 def dot(a, b):
@@ -78,7 +93,7 @@
     loads = [
         pltpu.make_async_copy(src, dst, load.at[i])
         for i, (src, dst) in enumerate((
-            (hid_h, hid), (dq_h, dq), (dv_h, dv), (kp_h, kp), (fv_h, fv), (uv_h, uv), (uq_h, uq), (qb_h, qb), (go_h, go),
+            (kp_h, kp), (hid_h, hid), (dq_h, dq), (dv_h, dv), (fv_h, fv), (uv_h, uv), (uq_h, uq), (qb_h, qb), (go_h, go),
         ))
     ]
     for copy in loads[:4]:
@@ -107,13 +122,8 @@
 
     for copy in loads[4:]:
         copy.start()
-    for copy in loads[:4]:
-        copy.wait()
-
-    down = jnp.concatenate([dq[...].astype(F32), dv[...].astype(F32)], axis=0).astype(BF16)
-    parts1[t] = dot_nt(down, hid[...])
+    loads[0].wait()
     kbuf[p] = kp[...]
-
     pl.semaphore_wait(barrier, (n_tensor - 1) + (group - 1) + 2 * (n_groups - 1))
 
     def part1_copy(i):
@@ -124,7 +134,6 @@
         part1_copy(i).start()
         return carry
 
-    lax.fori_loop(1, n_tensor, start_part1, 0)
 
     def k_copy(to):
         return remote(kp, kbuf.at[p], ks.at[to], kr.at[p], dev(g, 2 * to + yl))
@@ -144,13 +153,18 @@
     def v_wait(pp):
         arrived(vbuf.at[pp], vr.at[pp])
 
+    def start_k(to, carry):
+        k_copy(to).start()
+        return carry
+
+    lax.fori_loop(c + 1, chips, start_k, 0)
+
+    for copy in loads[1:4]:
+        copy.wait()
+    down = jnp.concatenate([dq[...].astype(F32), dv[...].astype(F32)], axis=0).astype(BF16)
+    parts1[t] = dot_nt(down, hid[...])
+    lax.fori_loop(1, n_tensor, start_part1, 0)
     k_pair(c).start()
-
-    def start_k(to, carry):
-        k_copy(chips - 1 - to).start()
-        return carry
-
-    lax.fori_loop(0, chips - 1 - c, start_k, 0)
 
     for copy in loads[4:]:
         copy.wait()
@@ -192,10 +206,10 @@
     v_pair(c).start()
 
     def start_v(to, carry):
-        v_copy(chips - 1 - to).start()
-        return carry
-
-    lax.fori_loop(0, chips - 1 - c, start_v, 0)
+        v_copy(to).start()
+        return carry
+
+    lax.fori_loop(c + 1, chips, start_v, 0)
 
     up_q = jnp.concatenate([uqf, none_q] * 3 + [jnp.zeros((TOK - 48, WIDTH), F32)], axis=0).astype(BF16)
     for h in range(HEADS):
@@ -216,8 +230,14 @@
         sbuf[c, rows, :] = sc
         stat[rows, :] = jnp.maximum(sc[:, :TOK], sc[:, TOK:])
 
-    def scores(i, carry):
+    def forward_v(i):
+        frm = c - 1 - i
+        v_wait(2 * frm + yl)
+        v_pair(frm).start()
+
+    def scores(i):
         ch = c - 1 - i
+
         k_wait(2 * ch + 1 - yl)
         kc = keys_of(ch)
         for h in range(HEADS):
@@ -225,21 +245,20 @@
             sc = dot_nt(qs[rows, :], kc) * (ROOT * LOG2E)
             sbuf[ch, rows, :] = sc
             stat[rows, :] = jnp.maximum(stat[rows, :], jnp.maximum(sc[:, :TOK], sc[:, TOK:]))
-        return carry
-
-    lax.fori_loop(0, c, scores, 0)
+
+    paced(c, scores, 2)
     for h in range(HEADS):
         rows = slice(h * TOK, (h + 1) * TOK)
         stat[rows, :] = jnp.broadcast_to(jnp.max(stat[rows, :], axis=1, keepdims=True), (TOK, HEAD))
     linv[...] = jnp.zeros_like(linv)
 
-    def exps(i, carry):
+    def exps(i):
         ch = c - i
+        ahead = i - 1
 
         @pl.when(i > 0)
         def _():
-            v_wait(2 * ch + yl)
-            v_pair(ch).start()
+            forward_v(ahead)
 
         for h in range(HEADS):
             rows = slice(h * TOK, (h + 1) * TOK)
@@ -249,9 +268,8 @@
             linv[rows, :] += e0 + e1
             ebuf[ch, rows, 0:TOK] = e0.astype(BF16)
             ebuf[ch, rows, TOK:2 * TOK] = e1.astype(BF16)
-        return carry
-
-    lax.fori_loop(0, c + 1, exps, 0)
+
+    paced(c + 1, exps, 2)
     for h in range(HEADS):
         rows = slice(h * TOK, (h + 1) * TOK)
         inv = 1.0 / jnp.sum(linv[rows, :], axis=1, keepdims=True)
@@ -265,7 +283,7 @@
     def lg_copy(to):
         return remote(lgout.at[to], lgin.at[p], ls.at[to], lr.at[p], dev(g, to))
 
-    def grads(i, carry):
+    def grads(i):
         ch = c - i
         both = dot(w16, ebuf[ch])
         lg = GAIN * (both[0:RANK] + both[RANK:2 * RANK])
@@ -280,24 +298,22 @@
         def _():
             lg_copy(2 * ch + 1).start()
 
-        return carry
-
-    lax.fori_loop(0, c + 1, grads, 0)
+    paced(c + 1, grads, 2)
 
     oacc[...] = jnp.zeros_like(oacc)
     dqacc[...] = jnp.zeros_like(dqacc)
 
-    def outs(i, carry):
+    def outs(i):
         ch = c - i
         v_wait(2 * ch + 1 - yl)
+
         vc = jnp.concatenate([vbuf[2 * ch, 0:TOK, :], vbuf[2 * ch + 1, 0:TOK, :]], axis=0)
         for h in range(HEADS):
             rows = slice(h * TOK, (h + 1) * TOK)
             oacc[rows, :] += dot(ebuf[ch, rows, :], vc)
             dpbuf[ch, rows, :] = dot_nt(go[:, rows], vc)
-        return carry
-
-    lax.fori_loop(0, c + 1, outs, 0)
+
+    paced(c + 1, outs, 2)
     for h in range(HEADS):
         rows = slice(h * TOK, (h + 1) * TOK)
         o = oacc[rows, :] * linv[rows, :]
@@ -311,18 +327,29 @@
     ]
     unloads[0].start()
 
-    def dquery(i, carry):
-        ch = c - i
-        kc = keys_of(ch)
+    def dquery(first, width):
+        kc = kbuf[pl.ds(2 * first, 2 * width)].reshape(2 * width * TOK, HEAD)
         for h in range(HEADS):
             rows = slice(h * TOK, (h + 1) * TOK)
             cen = stat[rows, :]
-            d0 = ebuf[ch, rows, 0:TOK].astype(F32) * (dpbuf[ch, rows, 0:TOK] - cen)
-            d1 = ebuf[ch, rows, TOK:2 * TOK].astype(F32) * (dpbuf[ch, rows, TOK:2 * TOK] - cen)
-            dqacc[rows, :] += dot(jnp.concatenate([d0.astype(BF16), d1.astype(BF16)], axis=1), kc)
-        return carry
-
-    lax.fori_loop(0, c + 1, dquery, 0)
+            ds = []
+            for j in range(width):
+                for half in (slice(0, TOK), slice(TOK, 2 * TOK)):
+                    part = dpbuf[first + j, rows, half] - cen
+                    ds.append((ebuf[first + j, rows, half].astype(F32) * part).astype(BF16))
+            dqacc[rows, :] += dot(jnp.concatenate(ds, axis=1), kc)
+
+    def dquery_four(i, carry):
+        dquery(4 * i, 4)
+        return carry
+
+    def dquery_one(i, carry):
+        dquery(i, 1)
+        return carry
+
+    fours = (c + 1) // 4
+    lax.fori_loop(0, fours, dquery_four, 0)
+    lax.fori_loop(4 * fours, c + 1, dquery_one, 0)
     for h in range(HEADS):
         rows = slice(h * TOK, (h + 1) * TOK)
         d_hi, d_lo = split2(dqacc[rows, :] * (linv[rows, :] * ROOT))
@@ -366,6 +393,29 @@
         if wide > HEAD:
             aout[k, 3 * RANK:4 * RANK, :] = jnp.zeros((RANK, wide), F32)
         aout[k, 3 * RANK:4 * RANK, 0:HEAD] = jnp.where(lax.rem(rank_row, chips) == k, g_up_v, 0.0)
+
+    def end_tensor(i, carry):
+        part1_copy(i).wait_send()
+        return carry
+
+    def end_row(to, carry):
+        k_copy(to).wait_send()
+        v_copy(to).wait_send()
+        return carry
+
+    def end_pair(frm, carry):
+        k_pair(frm).wait_send()
+        v_pair(frm).wait_send()
+        return carry
+
+    def end_lg(to, carry):
+        lg_copy(to).wait_send()
+        return carry
+
+    lax.fori_loop(1, n_tensor, end_tensor, 0)
+    lax.fori_loop(c + 1, chips, end_row, 0)
+    lax.fori_loop(0, c + 1, end_pair, 0)
+    lax.fori_loop(0, p, end_lg, 0)
 
     def wait_part2(i, carry):
         src = lax.rem(t + i, n_tensor)
@@ -432,6 +482,26 @@
         total = total + bin_[k]
     cin[c] = total
     lax.fori_loop(1, chips, start_c, 0)
+
+    def end_tensor2(i, carry):
+        part2_copy(i).wait_send()
+        return carry
+
+    def end_a(i, carry):
+        a_copy(i).wait_send()
+        return carry
+
+    def end_b(i, carry):
+        b_copy(i).wait_send()
+        return carry
+
+    def end_c(i, carry):
+        c_copy(i).wait_send()
+        return carry
+
+    lax.fori_loop(1, n_tensor, end_tensor2, 0)
+    lax.fori_loop(1, chips, end_a, 0)
+    lax.fori_loop(1, 2 * n_groups, end_b, 0)
     waiter(cin, crd, c, chips)
     up_total = jnp.zeros((RANK, HEAD), F32)
     for k in range(chips):
@@ -442,41 +512,8 @@
     guv[...] = up_total
     for copy in unloads[1:]:
         copy.start()
-
-    def end_tensor(i, carry):
-        part1_copy(i).wait_send()
-        part2_copy(i).wait_send()
-        return carry
-
-    def end_later(to, carry):
-        k_copy(to).wait_send()
-        v_copy(to).wait_send()
-        return carry
-
-    def end_pair(frm, carry):
-        k_pair(frm).wait_send()
-        v_pair(frm).wait_send()
-        return carry
-
-    def end_lg(to, carry):
-        lg_copy(to).wait_send()
-        return carry
-
-    def end_row(i, carry):
-        a_copy(i).wait_send()
-        c_copy(i).wait_send()
-        return carry
-
-    def end_far(i, carry):
-        b_copy(i).wait_send()
-        return carry
-
-    lax.fori_loop(1, n_tensor, end_tensor, 0)
-    lax.fori_loop(c + 1, chips, end_later, 0)
-    lax.fori_loop(0, c + 1, end_pair, 0)
-    lax.fori_loop(0, p, end_lg, 0)
-    lax.fori_loop(1, chips, end_row, 0)
-    lax.fori_loop(1, 2 * n_groups, end_far, 0)
+    lax.fori_loop(1, chips, end_c, 0)
+
     for copy in unloads:
         copy.wait()
 

time: 59.6 us -> 58.6 us (0.983)
  Pallas kernels: 58.8 us -> 57.8 us
    pallas_call x1, Pallas kernels: 57 us -> 56.1 us  [per_device(): pl.pallas_call(functools.partial(kernel, n_seq, n_tensor, group), out_sha...]
where the time goes in v3:
time: 58.6 us; the launch traced here: 58.5 us
  Pallas kernels  57.8 us (99%)
  between operations  0.64 us (1%)
    pallas_call x1, Pallas kernels, per_device(): pl.pallas_call(functools.partial(kernel, n_seq, n_tensor, group), out_sha...  56.1 us
    pallas_call x1, Pallas kernels, per_device(): pl.pallas_call(store, out_shape=results, in_specs=[hbm] * 5, out_specs=(h...  1.76 us

profile of v3, /device:TPU:6, one launch (start us, length us, event | category | flops | bytes accessed | tf_op | source)
XLA Modules:
  0.0 58.5 jit_solution(1040183276326730408)
XLA Ops:
  0.6 56.1 %shard_map.128 = (bf16[128,1024]{1,0:T(8,128)(2,1)}, f32[8,1024]{1,0:T(8,128)}, f32[8,1024]{1,0:T(8,128)}, f32[8,1024]{1,0:T(8,128)}, f32[8,128]{1,0:T(8,128)}) custom-call(bf16[128,1024]{1,0:T(8,128)(2,1)} %hid_h.1, bf16[128,1024]{1,0:T(8,128)(2,1)} %qb_h.1, bf16[128,128]{1,0:T(8,128)(2,1)} %kp_h.1, bf16[128,128]{1,0:T(8,128)(2,1)} %fv_h.1, ...), custom_call_target="tpu_custom_call" | custom-call | tf_op jit(solution)/shard_map/pallas_call | solution.py:553
  56.7 1.8 %shard_map.129 = (bf16[128,1024]{1,0:T(8,128)(2,1)}, f32[8,1024]{1,0:T(8,128)}, f32[8,1024]{1,0:T(8,128)}, f32[8,1024]{1,0:T(8,128)}, f32[8,128]{1,0:T(8,128)}) custom-call(bf16[128,1024]{1,0:T(8,128)(2,1)} %get-tuple-element.10.refs_0_, f32[8,1024]{1,0:T(8,128)} %get-tuple-element.11.refs_1_, f32[8,1024]{1,0:T(8,128)} %get-tuple-element.12.refs_2_, ...), custom_call_target="tpu_custom_call" | custom-call | tf_op jit(solution)/shard_map/pallas_call | solution.py:596

commit v4 on v3

--- a/solution.py
+++ b/solution.py
@@ -38,6 +38,11 @@
     lax.fori_loop(whole * width, count, rest, 0)
 
 
+def arrived_all(buf, sem, count):
+    if count > 1:
+        arrived(buf.at[pl.ds(0, count - 1)], sem.at[0])
+
+
 def dot(a, b):
     return jnp.dot(a, b, preferred_element_type=F32)
 
@@ -63,7 +68,7 @@
     hid, qb, kp, fv, dq, uq, dv, uv, go, load,
     parts1, parts2, kbuf, vbuf, vown, lgout, lgin, ain, bin_, cin, aout,
     qs, sbuf, ebuf, dpbuf, stat, linv, oacc, dqacc, dol, dqhi, dqlo,
-    p1s, p1r, ks, kf, kr, vs, vf, vr, ls, lr, p2s, p2r, asd, ard, bsd, brd, csd, crd,
+    p1s, p1r, ks, kf, kr, vs, vr, ls, lr, p2s, p2r, asd, ard, bsd, brd, csd, crd,
 ):
     s = lax.axis_index("seq")
     t = lax.axis_index("tensor")
@@ -124,46 +129,43 @@
         copy.start()
     loads[0].wait()
     kbuf[p] = kp[...]
-    pl.semaphore_wait(barrier, (n_tensor - 1) + (group - 1) + 2 * (n_groups - 1))
-
-    def part1_copy(i):
-        peer = lax.rem(t + i, n_tensor)
-        return remote(parts1.at[t], parts1.at[t], p1s.at[i], p1r.at[t], (s, peer))
-
-    def start_part1(i, carry):
-        part1_copy(i).start()
-        return carry
-
-
-    def k_copy(to):
-        return remote(kp, kbuf.at[p], ks.at[to], kr.at[p], dev(g, 2 * to + yl))
-
-    def k_pair(frm):
-        return remote(kbuf.at[2 * frm + yl], kbuf.at[2 * frm + yl], kf.at[frm], kr.at[2 * frm + yl], dev(g, mate))
-
-    def v_copy(to):
-        return remote(vown, vbuf.at[p], vs.at[to], vr.at[p], dev(g, 2 * to + yl))
-
-    def v_pair(frm):
-        return remote(vbuf.at[2 * frm + yl], vbuf.at[2 * frm + yl], vf.at[frm], vr.at[2 * frm + yl], dev(g, mate))
-
-    def k_wait(pp):
-        arrived(kbuf.at[pp], kr.at[pp])
-
-    def v_wait(pp):
-        arrived(vbuf.at[pp], vr.at[pp])
-
-    def start_k(to, carry):
-        k_copy(to).start()
-        return carry
-
-    lax.fori_loop(c + 1, chips, start_k, 0)
 
     for copy in loads[1:4]:
         copy.wait()
     down = jnp.concatenate([dq[...].astype(F32), dv[...].astype(F32)], axis=0).astype(BF16)
     parts1[t] = dot_nt(down, hid[...])
+    pl.semaphore_wait(barrier, (n_tensor - 1) + (group - 1) + 2 * (n_groups - 1))
+
+    def part1_copy(i):
+        peer = lax.rem(t + i, n_tensor)
+        return remote(parts1.at[t], parts1.at[t], p1s.at[0], p1r.at[0], (s, peer))
+
+    def start_part1(i, carry):
+        part1_copy(i).start()
+        return carry
+
+
+    def k_copy(to):
+        return remote(kp, kbuf.at[p], ks.at[to], kr.at[p], dev(g, 2 * to + yl))
+
+    def k_pair(frm):
+        return remote(kbuf.at[2 * frm + yl], kbuf.at[2 * frm + yl], kf.at[frm], kr.at[2 * frm + yl], dev(g, mate))
+
+    def v_copy(to):
+        return remote(vown, vbuf.at[p], vs.at[to], vr.at[p], dev(g, to))
+
+    def k_wait(pp):
+        arrived(kbuf.at[pp], kr.at[pp])
+
+    def v_wait(pp):
+        arrived(vbuf.at[pp], vr.at[pp])
+
     lax.fori_loop(1, n_tensor, start_part1, 0)
+    def start_k(to, carry):
+        k_copy(to).start()
+        return carry
+
+    lax.fori_loop(c + 1, chips, start_k, 0)
     k_pair(c).start()
 
     for copy in loads[4:]:
@@ -177,12 +179,14 @@
 
     lax.fori_loop(0, c, forward_k, 0)
 
-    def wait_part1(i, carry):
-        src = lax.rem(t + i, n_tensor)
-        arrived(parts1.at[src], p1r.at[src])
-        return carry
-
-    lax.fori_loop(1, n_tensor, wait_part1, 0)
+    none_q = jnp.zeros((RANK, WIDTH), F32)
+    none_v = jnp.zeros((RANK, HEAD), F32)
+    uqf = uq[...].astype(F32)
+    uvf = uv[...].astype(F32)
+    up_v = jnp.concatenate([none_v, uvf] * 3 + [jnp.zeros((TOK - 48, HEAD), F32)], axis=0).astype(BF16)
+    up_q = jnp.concatenate([uqf, none_q] * 3 + [jnp.zeros((TOK - 48, WIDTH), F32)], axis=0).astype(BF16)
+
+    arrived_all(parts1, p1r, n_tensor)
     low = parts1[0]
     for i in range(1, n_tensor):
         low = low + parts1[i]
@@ -192,26 +196,24 @@
     lo = rest - mid
     zeros = jnp.zeros((TOK - 48, TOK), F32)
     pieces = jnp.transpose(jnp.concatenate([hi, mid, lo, zeros], axis=0)).astype(BF16)
-    none_q = jnp.zeros((RANK, WIDTH), F32)
-    none_v = jnp.zeros((RANK, HEAD), F32)
-    uqf = uq[...].astype(F32)
-    uvf = uv[...].astype(F32)
-    up_v = jnp.concatenate([none_v, uvf] * 3 + [jnp.zeros((TOK - 48, HEAD), F32)], axis=0).astype(BF16)
     value = (fv[...].astype(F32) + GAIN * dot(pieces, up_v)).astype(BF16)
     low_v = jnp.concatenate([hi[RANK:], rest[RANK:]], axis=0).astype(BF16)
     vown[0:TOK, :] = value
     vown[TOK:TOK + 16, :] = low_v
     vbuf[p] = vown[...]
 
-    v_pair(c).start()
+    @pl.when(yl == 0)
+    def _():
+        vbuf[mate] = jnp.zeros((TOK + 16, HEAD), BF16)
+
 
     def start_v(to, carry):
         v_copy(to).start()
         return carry
 
-    lax.fori_loop(c + 1, chips, start_v, 0)
-
-    up_q = jnp.concatenate([uqf, none_q] * 3 + [jnp.zeros((TOK - 48, WIDTH), F32)], axis=0).astype(BF16)
+    lax.fori_loop(c + yl, chips, lambda i, q: start_v(2 * i + 1 - yl, q), 0)
+    lax.fori_loop(c + 1, chips, lambda i, q: start_v(2 * i + yl, q), 0)
+
     for h in range(HEADS):
         cols = slice(h * HEAD, (h + 1) * HEAD)
         qs[cols, :] = (qb[:, cols].astype(F32) + GAIN * dot(pieces, up_q[:, cols])).astype(BF16)
@@ -230,11 +232,6 @@
         sbuf[c, rows, :] = sc
         stat[rows, :] = jnp.maximum(sc[:, :TOK], sc[:, TOK:])
 
-    def forward_v(i):
-        frm = c - 1 - i
-        v_wait(2 * frm + yl)
-        v_pair(frm).start()
-
     def scores(i):
         ch = c - 1 - i
 
@@ -254,12 +251,6 @@
 
     def exps(i):
         ch = c - i
-        ahead = i - 1
-
-        @pl.when(i > 0)
-        def _():
-            forward_v(ahead)
-
         for h in range(HEADS):
             rows = slice(h * TOK, (h + 1) * TOK)
             m = stat[rows, :]
@@ -298,14 +289,22 @@
         def _():
             lg_copy(2 * ch + 1).start()
 
-    paced(c + 1, grads, 2)
+    paced(c + 1, grads, 4)
 
     oacc[...] = jnp.zeros_like(oacc)
     dqacc[...] = jnp.zeros_like(dqacc)
 
     def outs(i):
         ch = c - i
-        v_wait(2 * ch + 1 - yl)
+
+        @pl.when(i > 0)
+        def _():
+            v_wait(2 * ch)
+            v_wait(2 * ch + 1)
+
+        @pl.when(jnp.logical_and(i == 0, yl == 1))
+        def _():
+            v_wait(mate)
 
         vc = jnp.concatenate([vbuf[2 * ch, 0:TOK, :], vbuf[2 * ch + 1, 0:TOK, :]], axis=0)
         for h in range(HEADS):
@@ -313,7 +312,7 @@
             oacc[rows, :] += dot(ebuf[ch, rows, :], vc)
             dpbuf[ch, rows, :] = dot_nt(go[:, rows], vc)
 
-    paced(c + 1, outs, 2)
+    paced(c + 1, outs, 4)
     for h in range(HEADS):
         rows = slice(h * TOK, (h + 1) * TOK)
         o = oacc[rows, :] * linv[rows, :]
@@ -366,7 +365,7 @@
 
     def part2_copy(i):
         peer = lax.rem(t + i, n_tensor)
-        return remote(parts2.at[t], parts2.at[t], p2s.at[i], p2r.at[t], (s, peer))
+        return remote(parts2.at[t], parts2.at[t], p2s.at[0], p2r.at[0], (s, peer))
 
     def start_part2(i, carry):
         part2_copy(i).start()
@@ -394,35 +393,29 @@
             aout[k, 3 * RANK:4 * RANK, :] = jnp.zeros((RANK, wide), F32)
         aout[k, 3 * RANK:4 * RANK, 0:HEAD] = jnp.where(lax.rem(rank_row, chips) == k, g_up_v, 0.0)
 
-    def end_tensor(i, carry):
-        part1_copy(i).wait_send()
-        return carry
-
     def end_row(to, carry):
         k_copy(to).wait_send()
+        return carry
+
+    def end_v(to, carry):
         v_copy(to).wait_send()
         return carry
 
     def end_pair(frm, carry):
         k_pair(frm).wait_send()
-        v_pair(frm).wait_send()
         return carry
 
     def end_lg(to, carry):
         lg_copy(to).wait_send()
         return carry
 
-    lax.fori_loop(1, n_tensor, end_tensor, 0)
+    arrived_all(parts1, p1s, n_tensor)
     lax.fori_loop(c + 1, chips, end_row, 0)
     lax.fori_loop(0, c + 1, end_pair, 0)
+    lax.fori_loop(p + 1, group, end_v, 0)
     lax.fori_loop(0, p, end_lg, 0)
 
-    def wait_part2(i, carry):
-        src = lax.rem(t + i, n_tensor)
-        arrived(parts2.at[src], p2r.at[src])
-        return carry
-
-    lax.fori_loop(1, n_tensor, wait_part2, 0)
+    arrived_all(parts2, p2r, n_tensor)
     lowg = parts2[0]
     for i in range(1, n_tensor):
         lowg = lowg + parts2[i]
@@ -433,18 +426,18 @@
 
     def a_copy(i):
         to = lax.rem(c + i, chips)
-        return remote(aout.at[to], ain.at[c], asd.at[i], ard.at[c], dev(g, 2 * to + yl))
+        return remote(aout.at[to], ain.at[c], asd.at[0], ard.at[0], dev(g, 2 * to + yl))
 
     def c_copy(i):
         to = lax.rem(c + i, chips)
-        return remote(cin.at[c], cin.at[c], csd.at[i], crd.at[c], dev(g, 2 * to + yl))
+        return remote(cin.at[c], cin.at[c], csd.at[0], crd.at[0], dev(g, 2 * to + yl))
 
     mine = 2 * g + yl
 
     def b_copy(i):
         slot = lax.rem(mine + i, 2 * n_groups)
         return remote(
-            bin_.at[mine], bin_.at[mine], bsd.at[i], brd.at[mine],
+            bin_.at[mine], bin_.at[mine], bsd.at[0], brd.at[0],
             dev(slot // 2, 2 * c + lax.rem(slot, 2)),
         )
 
@@ -460,49 +453,25 @@
         c_copy(i).start()
         return carry
 
-    def waiter(buf, sem, me, count):
-        def body(i, carry):
-            src = lax.rem(me + i, count)
-            arrived(buf.at[src], sem.at[src])
-            return carry
-
-        lax.fori_loop(1, count, body, 0)
-
     lax.fori_loop(1, chips, start_a, 0)
     ain[c] = aout[c]
-    waiter(ain, ard, c, chips)
+    arrived_all(ain, ard, chips)
     total = ain[0]
     for k in range(1, chips):
         total = total + ain[k]
     bin_[mine] = total
     lax.fori_loop(1, 2 * n_groups, start_b, 0)
-    waiter(bin_, brd, mine, 2 * n_groups)
+    arrived_all(bin_, brd, 2 * n_groups)
     total = bin_[0]
     for k in range(1, 2 * n_groups):
         total = total + bin_[k]
     cin[c] = total
     lax.fori_loop(1, chips, start_c, 0)
 
-    def end_tensor2(i, carry):
-        part2_copy(i).wait_send()
-        return carry
-
-    def end_a(i, carry):
-        a_copy(i).wait_send()
-        return carry
-
-    def end_b(i, carry):
-        b_copy(i).wait_send()
-        return carry
-
-    def end_c(i, carry):
-        c_copy(i).wait_send()
-        return carry
-
-    lax.fori_loop(1, n_tensor, end_tensor2, 0)
-    lax.fori_loop(1, chips, end_a, 0)
-    lax.fori_loop(1, 2 * n_groups, end_b, 0)
-    waiter(cin, crd, c, chips)
+    arrived_all(parts2, p2s, n_tensor)
+    arrived_all(aout, asd, chips)
+    arrived_all(bin_, bsd, 2 * n_groups)
+    arrived_all(cin, crd, chips)
     up_total = jnp.zeros((RANK, HEAD), F32)
     for k in range(chips):
         gdq[:, k * wide:(k + 1) * wide] = cin[k, 0:RANK, :]
@@ -512,7 +481,7 @@
     guv[...] = up_total
     for copy in unloads[1:]:
         copy.start()
-    lax.fori_loop(1, chips, end_c, 0)
+    arrived_all(cin, csd, chips)
 
     for copy in unloads:
         copy.wait()
@@ -582,7 +551,7 @@
                 pltpu.VMEM((TOK, WIDTH), BF16),
                 dma((n_tensor,)), dma((n_tensor,)),
                 dma((chips,)), dma((chips,)), dma((group,)),
-                dma((chips,)), dma((chips,)), dma((group,)),
+                dma((group,)), dma((group,)),
                 dma((group,)), dma((group,)),
                 dma((n_tensor,)), dma((n_tensor,)),
                 dma((chips,)), dma((chips,)),

time: 58.6 us -> 58.3 us (level)
  Pallas kernels: 57.8 us -> 57.2 us
    pallas_call x1, Pallas kernels: 56.1 us -> 55.4 us  [per_device(): pl.pallas_call(functools.partial(kernel, n_seq, n_tensor, group), out_sha...]
where the time goes in v4:
time: 58.3 us; the launch traced here: 57.8 us
  Pallas kernels  57.2 us (98%)
  between operations  0.64 us (1%)
    pallas_call x1, Pallas kernels, per_device(): pl.pallas_call(functools.partial(kernel, n_seq, n_tensor, group), out_sha...  55.4 us
    pallas_call x1, Pallas kernels, per_device(): pl.pallas_call(store, out_shape=results, in_specs=[hbm] * 5, out_specs=(h...  1.76 us

profile of v4, /device:TPU:6, one launch (start us, length us, event | category | flops | bytes accessed | tf_op | source)
XLA Modules:
  0.0 57.8 jit_solution(6412496004978244944)
XLA Ops:
  0.6 55.4 %shard_map.128 = (bf16[128,1024]{1,0:T(8,128)(2,1)}, f32[8,1024]{1,0:T(8,128)}, f32[8,1024]{1,0:T(8,128)}, f32[8,1024]{1,0:T(8,128)}, f32[8,128]{1,0:T(8,128)}) custom-call(bf16[128,1024]{1,0:T(8,128)(2,1)} %hid_h.1, bf16[128,1024]{1,0:T(8,128)(2,1)} %qb_h.1, bf16[128,128]{1,0:T(8,128)(2,1)} %kp_h.1, bf16[128,128]{1,0:T(8,128)(2,1)} %fv_h.1, ...), custom_call_target="tpu_custom_call" | custom-call | tf_op jit(solution)/shard_map/pallas_call | solution.py:522
  56.0 1.8 %shard_map.129 = (bf16[128,1024]{1,0:T(8,128)(2,1)}, f32[8,1024]{1,0:T(8,128)}, f32[8,1024]{1,0:T(8,128)}, f32[8,1024]{1,0:T(8,128)}, f32[8,128]{1,0:T(8,128)}) custom-call(bf16[128,1024]{1,0:T(8,128)(2,1)} %get-tuple-element.10.refs_0_, f32[8,1024]{1,0:T(8,128)} %get-tuple-element.11.refs_1_, f32[8,1024]{1,0:T(8,128)} %get-tuple-element.12.refs_2_, ...), custom_call_target="tpu_custom_call" | custom-call | tf_op jit(solution)/shard_map/pallas_call | solution.py:565

commit v5 on v4

--- a/solution.py
+++ b/solution.py
@@ -243,7 +243,7 @@
             sbuf[ch, rows, :] = sc
             stat[rows, :] = jnp.maximum(stat[rows, :], jnp.maximum(sc[:, :TOK], sc[:, TOK:]))
 
-    paced(c, scores, 2)
+    paced(c, scores, 4)
     for h in range(HEADS):
         rows = slice(h * TOK, (h + 1) * TOK)
         stat[rows, :] = jnp.broadcast_to(jnp.max(stat[rows, :], axis=1, keepdims=True), (TOK, HEAD))

time: 58.3 us -> 58.3 us (level)
  no operation moved by 1% of the time
where the time goes in v5:
time: 58.3 us; the launch traced here: 57.8 us
  Pallas kernels  57.2 us (98%)
  between operations  0.64 us (1%)
    pallas_call x1, Pallas kernels, per_device(): pl.pallas_call(functools.partial(kernel, n_seq, n_tensor, group), out_sha...  55.4 us
    pallas_call x1, Pallas kernels, per_device(): pl.pallas_call(store, out_shape=results, in_specs=[hbm] * 5, out_specs=(h...  1.76 us

profile of v5, /device:TPU:6, one launch (start us, length us, event | category | flops | bytes accessed | tf_op | source)
XLA Modules:
  0.0 57.8 jit_solution(9047789107405973609)
XLA Ops:
  0.6 55.4 %shard_map.128 = (bf16[128,1024]{1,0:T(8,128)(2,1)}, f32[8,1024]{1,0:T(8,128)}, f32[8,1024]{1,0:T(8,128)}, f32[8,1024]{1,0:T(8,128)}, f32[8,128]{1,0:T(8,128)}) custom-call(bf16[128,1024]{1,0:T(8,128)(2,1)} %hid_h.1, bf16[128,1024]{1,0:T(8,128)(2,1)} %qb_h.1, bf16[128,128]{1,0:T(8,128)(2,1)} %kp_h.1, bf16[128,128]{1,0:T(8,128)(2,1)} %fv_h.1, ...), custom_call_target="tpu_custom_call" | custom-call | tf_op jit(solution)/shard_map/pallas_call | solution.py:522
  56.0 1.8 %shard_map.129 = (bf16[128,1024]{1,0:T(8,128)(2,1)}, f32[8,1024]{1,0:T(8,128)}, f32[8,1024]{1,0:T(8,128)}, f32[8,1024]{1,0:T(8,128)}, f32[8,128]{1,0:T(8,128)}) custom-call(bf16[128,1024]{1,0:T(8,128)(2,1)} %get-tuple-element.10.refs_0_, f32[8,1024]{1,0:T(8,128)} %get-tuple-element.11.refs_1_, f32[8,1024]{1,0:T(8,128)} %get-tuple-element.12.refs_2_, ...), custom_call_target="tpu_custom_call" | custom-call | tf_op jit(solution)/shard_map/pallas_call | solution.py:565
